TPU v7x, 256 devices: a whole 4x4x8 slice. The times are simulated.
256 devices in a mesh: seq: 16 (over z, core), own: 16 (over x, y).
Axes of the slice: x: 4, y: 4, z: 8, core: 2. Of those that a mesh axis runs over, the one named last changes fastest.
Arguments:
- query_rows: bfloat16 [16, 2048, 2048], P('own', 'seq'), may hold values from -9 to 9
- key_rows: bfloat16 [16, 2048, 2048], P('own', 'seq'), may hold values from -9 to 9
- value_rows: bfloat16 [16, 2048, 2048], P('own', 'seq'), may hold values from -16 to 16
- out_grad: bfloat16 [16, 2048, 2048], P('own', 'seq'), may hold values from -6 to 6
- norm_gains: float32 [2048], P('own'), may hold values from 0.1 to 1.9
- window: int32 [16], P('seq'), may hold values from 0 to 2, as said below
- global_blocks: int32 [16, 2], P('own'), may hold values from 0 to 31, as said below
- random_blocks: int32 [16, 32, 3], P('seq'), may hold values from 0 to 31
Outputs:
- grad_q: bfloat16 [16, 2048, 2048], P('own', 'seq')
- grad_k: bfloat16 [16, 2048, 2048], P('own', 'seq')
- grad_v: bfloat16 [16, 2048, 2048], P('own', 'seq')
- gain_grad: float32 [2048], P('seq')
Inputs may be any that keep to these rules, and one draw needn't show every extreme that they name: `window`: some head reaches 2 blocks on either side in every draw. `global_blocks`: the 2 global blocks of a filing are distinct.
All inputs are finite; a program needn't handle non-finite values.
Results may differ from a plain program's by a relative error of at most 0.012.
Values may be sent and summed in bfloat16 or wider, within the bound.
No kernel may reach another device: no remote copies, remote signals or barrier semaphores. Data moves between devices by JAX's collectives and lax.ppermute only.
A program may use at most 128 MiB of HBM per device.

v0:
```python
import functools
import math

import jax
import jax.numpy as jnp
from jax import lax
from jax.experimental import pallas as pl
from jax.experimental.pallas import tpu as pltpu
from jax.sharding import PartitionSpec as P

HDIM = 128
BLK = 64
NEG_FILL = -1e30
EPSILON = 1e-05
QTILE = 256
KTILE = 256
VMEM_LIMIT = 48 * 1024 * 1024


def pack_kernel(q_ref, k_ref, v_ref, g_ref, out_ref):
    heads = out_ref.shape[0]
    rows = q_ref.shape[1]
    for slot, ref in enumerate((q_ref, k_ref, v_ref, g_ref)):
        for h in range(heads):
            out_ref[h, slot * rows:(slot + 1) * rows, :] = ref[0, :, h * HDIM:(h + 1) * HDIM]


def pack(query_rows, key_rows, value_rows, out_grad):
    _, rows, cols = query_rows.shape
    heads = cols // HDIM
    steps = 4
    spec = pl.BlockSpec((1, rows, cols // steps), lambda i: (0, 0, i))
    return pl.pallas_call(
        pack_kernel,
        grid=(steps,),
        out_shape=jax.ShapeDtypeStruct((heads, 4 * rows, HDIM), query_rows.dtype),
        in_specs=[spec] * 4,
        out_specs=pl.BlockSpec((heads // steps, 4 * rows, HDIM), lambda i: (i, 0, 0)),
        name="pack",
    )(query_rows, key_rows, value_rows, out_grad)


def unpack_kernel(in_ref, q_ref, k_ref, v_ref):
    heads = in_ref.shape[0]
    rows = q_ref.shape[1]
    for slot, ref in enumerate((q_ref, k_ref, v_ref)):
        for h in range(heads):
            ref[0, :, h * HDIM:(h + 1) * HDIM] = in_ref[h, slot * rows:(slot + 1) * rows, :]


def unpack(exchanged):
    heads, rows3, _ = exchanged.shape
    rows = rows3 // 3
    steps = 4
    spec = pl.BlockSpec((1, rows, heads * HDIM // steps), lambda i: (0, 0, i))
    shape = jax.ShapeDtypeStruct((1, rows, heads * HDIM), exchanged.dtype)
    return pl.pallas_call(
        unpack_kernel,
        grid=(steps,),
        out_shape=[shape] * 3,
        in_specs=[pl.BlockSpec((heads // steps, rows3, HDIM), lambda i: (i, 0, 0))],
        out_specs=[spec] * 3,
        name="unpack",
    )(exchanged)


def forward_kernel(
    q_ref, k_ref, v_ref, g_ref, bias_ref, gain_ref,
    e_ref, attn_ref, inv_ref, stat_ref,
    vt_ref, s_ref,
):
    seq = s_ref.shape[0]
    devs = stat_ref.shape[0]

    @pl.when(pl.program_id(0) == 0)
    def _():
        for i in range(v_ref.shape[0]):
            vt_ref[:, i * 128:(i + 1) * 128] = v_ref[i].astype(jnp.float32).T.astype(jnp.bfloat16)

    q = q_ref[...].reshape(QTILE, HDIM)
    top = jnp.full((8, QTILE), NEG_FILL, jnp.float32)
    for c in range(seq // KTILE):
        keys = k_ref[c * 2:(c + 1) * 2].reshape(KTILE, HDIM)
        s = lax.dot_general(keys, q, (((1,), (1,)), ((), ())), preferred_element_type=jnp.float32)
        for b in range(KTILE // BLK):
            row = c * (KTILE // BLK) + b
            sb = s[b * BLK:(b + 1) * BLK] + bias_ref[row:row + 1, :]
            s_ref[row * BLK:(row + 1) * BLK, :] = sb
            top = jnp.maximum(top, jnp.max(sb.reshape(BLK // 8, 8, QTILE), axis=0))
    top = jnp.max(top, axis=0, keepdims=True)
    factor = math.log2(math.e) / math.sqrt(HDIM)
    total = jnp.zeros((8, QTILE), jnp.float32)
    for c in range(seq // KTILE):
        e = jnp.exp2((s_ref[c * KTILE:(c + 1) * KTILE, :] - top) * factor)
        total = total + jnp.sum(e.reshape(KTILE // 8, 8, QTILE), axis=0)
        e_ref[c * KTILE:(c + 1) * KTILE, :] = e.astype(jnp.bfloat16)
    inv = 1.0 / jnp.sum(total, axis=0, keepdims=True)
    attn = jnp.dot(vt_ref[...], e_ref[...], preferred_element_type=jnp.float32) * inv
    attn = attn.astype(jnp.bfloat16)
    attn_ref[...] = attn
    inv_ref[...] = inv
    attn = attn.astype(jnp.float32)
    grad = g_ref[...].reshape(QTILE, HDIM).astype(jnp.float32).T
    stats = jnp.concatenate(
        [
            jnp.sum(attn * attn, axis=0, keepdims=True),
            jnp.sum(gain_ref[...] * grad * attn, axis=0, keepdims=True),
        ],
        axis=0,
    )
    for d in range(devs):
        stat_ref[d] = stats


def forward(exchanged, bias, gain_col):
    devs, rows4, _ = exchanged.shape
    rows = rows4 // 4
    seq = devs * rows
    per = QTILE // rows
    whole = lambda slot: pl.BlockSpec((devs, rows, HDIM), lambda j: (0, slot, 0))
    part = lambda slot: pl.BlockSpec((per, rows, HDIM), lambda j: (j, slot, 0))
    return pl.pallas_call(
        forward_kernel,
        grid=(seq // QTILE,),
        out_shape=[
            jax.ShapeDtypeStruct((seq, seq), jnp.bfloat16),
            jax.ShapeDtypeStruct((HDIM, seq), jnp.bfloat16),
            jax.ShapeDtypeStruct((1, seq), jnp.float32),
            jax.ShapeDtypeStruct((devs, 2, seq), jnp.float32),
        ],
        in_specs=[
            part(0), whole(1), whole(2), part(3),
            pl.BlockSpec((seq // BLK, QTILE), lambda j: (0, j)),
            pl.BlockSpec((HDIM, 1), lambda j: (0, 0)),
        ],
        out_specs=[
            pl.BlockSpec((seq, QTILE), lambda j: (0, j)),
            pl.BlockSpec((HDIM, QTILE), lambda j: (0, j)),
            pl.BlockSpec((1, QTILE), lambda j: (0, j)),
            pl.BlockSpec((devs, 2, QTILE), lambda j: (0, 0, j)),
        ],
        scratch_shapes=[
            pltpu.VMEM((HDIM, seq), jnp.bfloat16),
            pltpu.VMEM((seq, QTILE), jnp.float32),
        ],
        compiler_params=pltpu.CompilerParams(vmem_limit_bytes=VMEM_LIMIT),
        name="forward",
    )(exchanged, exchanged, exchanged, exchanged, bias, gain_col)


def backward_kernel(
    q_ref, k_ref, v_ref, g_ref, e_ref, attn_ref, inv_ref, stat_ref, gain_ref,
    out_ref, gain_out_ref,
    kt_ref, ds_ref, dk_ref, dv_ref,
):
    j = pl.program_id(0)
    devs, rows, _ = k_ref.shape
    seq = devs * rows
    cols = seq
    scale = 1.0 / math.sqrt(HDIM)

    @pl.when(j == 0)
    def _():
        for i in range(devs):
            kt_ref[:, i * 128:(i + 1) * 128] = k_ref[i].astype(jnp.float32).T.astype(jnp.bfloat16)
        dk_ref[...] = jnp.zeros_like(dk_ref)
        dv_ref[...] = jnp.zeros_like(dv_ref)
        gain_out_ref[...] = jnp.zeros_like(gain_out_ref)

    width = devs * HDIM
    stats = jnp.sum(stat_ref[...], axis=0) * (1.0 / width)
    inv_rms = lax.rsqrt(stats[0:1] + EPSILON)
    inner = stats[1:2]
    attn = attn_ref[...].astype(jnp.float32)
    grad = g_ref[...].reshape(QTILE, HDIM).astype(jnp.float32).T
    q = q_ref[...].reshape(QTILE, HDIM)
    attn_grad = inv_rms * (gain_ref[...] * grad - attn * (inv_rms * inv_rms) * inner)
    gain_out_ref[...] += jnp.sum(grad * attn * inv_rms, axis=1, keepdims=True)
    low = (attn_grad * inv_ref[...]).astype(jnp.bfloat16)
    row_dot = jnp.sum(low.astype(jnp.float32) * attn, axis=0, keepdims=True)
    for c in range(seq // KTILE):
        span = slice(c * KTILE, (c + 1) * KTILE)
        e = e_ref[span, :]
        values = v_ref[c * 2:(c + 1) * 2].reshape(KTILE, HDIM)
        dp = jnp.dot(values, low, preferred_element_type=jnp.float32)
        ds = (e.astype(jnp.float32) * (dp - row_dot)).astype(jnp.bfloat16)
        ds_ref[span, :] = ds
        dk_ref[span, :] += jnp.dot(ds, q, preferred_element_type=jnp.float32)
        dv_ref[span, :] += lax.dot_general(
            e, low, (((1,), (1,)), ((), ())), preferred_element_type=jnp.float32
        )
    dq = jnp.dot(kt_ref[...], ds_ref[...], preferred_element_type=jnp.float32) * scale
    dq = dq.T.astype(jnp.bfloat16)
    per = QTILE // rows
    for i in range(per):
        out_ref[j * per + i, 0:rows, :] = dq[i * rows:(i + 1) * rows]

    @pl.when(j == pl.num_programs(0) - 1)
    def _():
        for i in range(devs):
            span = slice(i * rows, (i + 1) * rows)
            out_ref[i, rows:2 * rows, :] = (dk_ref[span, :] * scale).astype(jnp.bfloat16)
            out_ref[i, 2 * rows:3 * rows, :] = dv_ref[span, :].astype(jnp.bfloat16)


def backward(exchanged, weights, attn_t, inv_sum, stats, gain_col):
    devs, rows4, _ = exchanged.shape
    rows = rows4 // 4
    seq = devs * rows
    per = QTILE // rows
    whole = lambda slot: pl.BlockSpec((devs, rows, HDIM), lambda j: (0, slot, 0))
    part = lambda slot: pl.BlockSpec((per, rows, HDIM), lambda j: (j, slot, 0))
    return pl.pallas_call(
        backward_kernel,
        grid=(seq // QTILE,),
        out_shape=[
            jax.ShapeDtypeStruct((devs, 3 * rows, HDIM), jnp.bfloat16),
            jax.ShapeDtypeStruct((HDIM, 1), jnp.float32),
        ],
        in_specs=[
            part(0), whole(1), whole(2), part(3),
            pl.BlockSpec((seq, QTILE), lambda j: (0, j)),
            pl.BlockSpec((HDIM, QTILE), lambda j: (0, j)),
            pl.BlockSpec((1, QTILE), lambda j: (0, j)),
            pl.BlockSpec((devs, 2, QTILE), lambda j: (0, 0, j)),
            pl.BlockSpec((HDIM, 1), lambda j: (0, 0)),
        ],
        out_specs=[
            pl.BlockSpec((devs, 3 * rows, HDIM), lambda j: (0, 0, 0)),
            pl.BlockSpec((HDIM, 1), lambda j: (0, 0)),
        ],
        scratch_shapes=[
            pltpu.VMEM((HDIM, seq), jnp.bfloat16),
            pltpu.VMEM((seq, QTILE), jnp.bfloat16),
            pltpu.VMEM((seq, HDIM), jnp.float32),
            pltpu.VMEM((seq, HDIM), jnp.float32),
        ],
        compiler_params=pltpu.CompilerParams(vmem_limit_bytes=VMEM_LIMIT),
        name="backward",
    )(exchanged, exchanged, exchanged, exchanged, weights, attn_t, inv_sum, stats, gain_col)


def mask_bias(head_width, filing_globals, head_random, seq):
    count = seq // BLK
    keys = jnp.arange(count, dtype=jnp.int32)[:, None]
    queries = jnp.arange(count, dtype=jnp.int32)[None, :]
    allowed = jnp.abs(keys - queries) <= head_width
    for g in range(filing_globals.shape[0]):
        allowed = allowed | (keys == filing_globals[g]) | (queries == filing_globals[g])
    for r in range(head_random.shape[1]):
        allowed = allowed | (keys == head_random[:, r][None, :])
    return jnp.repeat(jnp.where(allowed, 0.0, NEG_FILL).astype(jnp.float32), BLK, axis=1)


def body(
    query_rows, key_rows, value_rows, out_grad, norm_gains, window, global_blocks, random_blocks
):
    seq_count = lax.axis_size("seq")
    own_count = lax.axis_size("own")
    rows = query_rows.shape[1]
    seq = rows * seq_count
    gain_scale = (own_count * seq) ** (-0.5)
    exchange = functools.partial(
        lax.all_to_all, axis_name="seq", split_axis=0, concat_axis=0, tiled=True
    )
    packed = pack(query_rows, key_rows, value_rows, out_grad)
    exchanged = exchange(packed)
    swap = [(o * own_count + s, s * own_count + o) for s in range(seq_count) for o in range(own_count)]
    gain_col = lax.ppermute(norm_gains, ("seq", "own"), swap).reshape(-1, 1)
    bias = mask_bias(window[0], global_blocks[0], random_blocks[0], seq)
    weights, attn_t, inv_sum, stats = forward(exchanged, bias, gain_col)
    stats = exchange(stats)
    grads, gain_part = backward(exchanged, weights, attn_t, inv_sum, stats, gain_col)
    gain_terms = lax.all_gather(gain_part.reshape(-1), "own")
    gain_grad = jnp.sum(gain_terms, axis=0) * gain_scale
    out_query, out_key, out_value = unpack(exchange(grads))
    return (out_query, out_key, out_value, gain_grad)


def solution(mesh):
    rows = P("own", "seq", None)
    placed = (rows, rows, rows, rows, P("own"), P("seq"), P("own", None), P("seq", None, None))
    return jax.shard_map(
        body,
        mesh=mesh,
        in_specs=placed,
        out_specs=(rows, rows, rows, P("seq")),
        check_vma=False,
    )
```

profile of v0, /device:TPU:1, one launch (start us, length us, event | category | flops | bytes accessed | tf_op | source)
XLA Modules:
  0.0 164.6 jit_solution(16355124098702142649)
XLA Ops:
  0.6 4.0 %pack.1 = bf16[16,512,128]{2,1,0:T(8,128)(2,1)} custom-call(bf16[1,128,2048]{2,1,0:T(8,128)(2,1)} %q_ref.1, bf16[1,128,2048]{2,1,0:T(8,128)(2,1)} %k_ref.1, bf16[1,128,2048]{2,1,0:T(8,128)(2,1)} %v_ref.1, bf16[1,128,2048]{2,1,0:T(8,128)(2,1)} %g_ref.1), custom_call_target="tpu_custom_call" | custom-call | tf_op jit(solution)/shard_map/pack/pallas_call | solution.py:33
  4.6 0.0 copy-start.4
  4.6 0.0 copy-start.3
  4.6 0.0 copy-start.2
  4.6 10.1 %all-to-all-start = ((bf16[16,512,128]{2,1,0:T(8,128)(2,1)}), bf16[16,512,128]{2,1,0:T(8,128)(2,1)S(1)}, u32[]{:S(2)}, u32[]{:S(2)}) async-start(bf16[16,512,128]{2,1,0:T(8,128)(2,1)} %pack.1), calls=%async_computation | async-start | bytes 4194304 | tf_op jit(solution)/shard_map/all_to_all | solution.py:267
  14.7 0.0 copy-done.4
  14.7 3.2 %collective-permute-start = (f32[128]{0:T(128)S(1)}, f32[128]{0:T(128)S(1)}, u32[]{:S(2)}, u32[]{:S(2)}) collective-permute-start(f32[128]{0:T(128)S(1)} %copy-done.4), channel_id=1, source_target_pairs={{0,0},{16,1},{32,2},{48,3},{64,4},{80,5},{96,6},{112,7},{128,8},{1... | collective-permute-start | bytes 1544 | tf_op jit(solution)/shard_map/ppermute | solution.py:269
  18.6 0.0 copy-done.3
  18.6 0.0 copy-done.2
  18.6 0.6 fusion.8
  19.2 1.3 iota_compare_fusion.3
  20.5 0.1 fusion.7
  20.6 0.2 broadcast_in_dim.15
  20.8 0.2 reshape.41.bias_ref
  21.0 0.0 collective-permute-done
  21.0 0.1 copy.14.gain_ref
  21.1 42.6 %all-to-all-done.q_ref.k_ref.v_ref.g_ref = bf16[16,512,128]{2,1,0:T(8,128)(2,1)S(1)} async-done(((bf16[16,512,128]{2,1,0:T(8,128)(2,1)}), bf16[16,512,128]{2,1,0:T(8,128)(2,1)S(1)}, u32[]{:S(2)}, u32[]{:S(2)}) %all-to-all-start) | async-done | bytes 2097184 | tf_op jit(solution)/shard_map/all_to_all | solution.py:267
  63.7 13.1 %forward.1 = (bf16[2048,2048]{1,0:T(8,128)(2,1)}, bf16[128,2048]{1,0:T(8,128)(2,1)S(1)}, f32[1,2048]{1,0:T(1,128)S(1)}, f32[16,2,2048]{2,1,0:T(2,128)S(1)}) custom-call(bf16[16,512,128]{2,1,0:T(8,128)(2,1)S(1)} %all-to-all-done.q_ref.k_ref.v_ref.g_ref, bf16[16,512,128]{2,1,0:T(8,128)(2,1)S(1)} %all-to-all-done.q_ref.k_ref.v_ref.g_ref, ...), custom_call_target="tpu_custom_call" | custom-call | tf_op jit(solution)/shard_map/forward/pallas_call | solution.py:122
  76.8 20.6 %all_to_all.15.stat_ref = f32[16,2,2048]{2,1,0:T(2,128)S(1)} all-to-all(f32[16,2,2048]{2,1,0:T(2,128)S(1)} %get-tuple-element.16), channel_id=1, replica_groups=mesh['seq'=16,'own'=16] {'seq'}, dimensions={0} | all-to-all | bytes 524288 | tf_op jit(solution)/shard_map/all_to_all | solution.py:272
  97.4 19.8 %backward.1 = (bf16[16,384,128]{2,1,0:T(8,128)(2,1)S(1)}, f32[128,1]{1,0:T(8,128)S(1)}) custom-call(bf16[16,512,128]{2,1,0:T(8,128)(2,1)S(1)} %all-to-all-done.q_ref.k_ref.v_ref.g_ref, bf16[16,512,128]{2,1,0:T(8,128)(2,1)S(1)} %all-to-all-done.q_ref.k_ref.v_ref.g_ref, bf16[16,512,128]{2,1,0:T(8,128)(2,1)S(1)} %all-to-all-done.q_ref.k_ref.v_ref.g_ref, ...), custom_call_target="tpu_custom_call" | custom-call | tf_op jit(solution)/shard_map/backward/pallas_call | solution.py:213
  117.2 0.0 copy-start
  117.2 1.1 copy-done
  118.3 3.6 %all-to-all-start.2 = ((bf16[16,384,128]{2,1,0:T(8,128)(2,1)}), bf16[16,384,128]{2,1,0:T(8,128)(2,1)S(1)}, u32[]{:S(2)}, u32[]{:S(2)}) async-start(bf16[16,384,128]{2,1,0:T(8,128)(2,1)} %copy-done), calls=%async_computation.2 | async-start | bytes 3145728 | tf_op jit(solution)/shard_map/all_to_all | solution.py:276
  121.9 20.0 %all-gather = f32[2048,1]{1,0:T(8,128)S(1)} all-gather(f32[128,1]{1,0:T(8,128)S(1)} %get-tuple-element.21), channel_id=2, replica_groups=mesh['seq'=16,'own'=16] {'own'}, dimensions={0}, use_global_device_ids=true | all-gather | bytes 8704 | tf_op jit(solution)/shard_map/all_gather | solution.py:274
  141.9 0.3 reduce
  142.3 0.5 broadcast_multiply_fusion
  142.8 17.0 %all-to-all-done.2.in_ref = bf16[16,384,128]{2,1,0:T(8,128)(2,1)S(1)} async-done(((bf16[16,384,128]{2,1,0:T(8,128)(2,1)}), bf16[16,384,128]{2,1,0:T(8,128)(2,1)S(1)}, u32[]{:S(2)}, u32[]{:S(2)}) %all-to-all-start.2) | async-done | bytes 1572896 | tf_op jit(solution)/shard_map/all_to_all | solution.py:276
  159.8 0.0 copy-start.1
  159.8 1.1 copy-done.1
  160.9 3.6 %unpack.1 = (bf16[1,128,2048]{2,1,0:T(8,128)(2,1)}, bf16[1,128,2048]{2,1,0:T(8,128)(2,1)}, bf16[1,128,2048]{2,1,0:T(8,128)(2,1)}) custom-call(bf16[16,384,128]{2,1,0:T(8,128)(2,1)} %copy-done.1), custom_call_target="tpu_custom_call" | custom-call | tf_op jit(solution)/shard_map/unpack/pallas_call | solution.py:57
  (3 shorter events, 0.0 us)
Async XLA Ops:
  4.6 10.1 %copy-start.4 = (f32[128]{0:T(128)S(1)}, f32[128]{0:T(128)}, u32[]{:S(2)}) copy-start(f32[128]{0:T(128)} %param.12) | copy-start | bytes 1540
  4.6 14.0 %copy-start.3 = (s32[1,32,3]{1,0,2:T(1,128)S(1)}, s32[1,32,3]{1,0,2:T(1,128)}, u32[]{:S(2)}) copy-start(s32[1,32,3]{1,0,2:T(1,128)} %param.15) | copy-start | bytes 1156
  4.6 14.0 %copy-start.2 = (s32[1,2]{1,0:T(1,128)S(1)}, s32[1,2]{1,0:T(1,128)}, u32[]{:S(2)}) copy-start(s32[1,2]{1,0:T(1,128)} %param.14) | copy-start | bytes 28
  4.6 59.1 %all-to-all-start = ((bf16[16,512,128]{2,1,0:T(8,128)(2,1)}), bf16[16,512,128]{2,1,0:T(8,128)(2,1)S(1)}, u32[]{:S(2)}, u32[]{:S(2)}) async-start(bf16[16,512,128]{2,1,0:T(8,128)(2,1)} %pack.1), calls=%async_computation | async-start | bytes 4194304 | tf_op jit(solution)/shard_map/all_to_all | solution.py:267
  14.7 6.3 %collective-permute-start = (f32[128]{0:T(128)S(1)}, f32[128]{0:T(128)S(1)}, u32[]{:S(2)}, u32[]{:S(2)}) collective-permute-start(f32[128]{0:T(128)S(1)} %copy-done.4), channel_id=1, source_target_pairs={{0,0},{16,1},{32,2},{48,3},{64,4},{80,5},{96,6},{112,7},{128,8},{1... | collective-permute-start | bytes 1544 | tf_op jit(solution)/shard_map/ppermute | solution.py:269
  117.2 1.2 copy-start
  118.3 41.5 %all-to-all-start.2 = ((bf16[16,384,128]{2,1,0:T(8,128)(2,1)}), bf16[16,384,128]{2,1,0:T(8,128)(2,1)S(1)}, u32[]{:S(2)}, u32[]{:S(2)}) async-start(bf16[16,384,128]{2,1,0:T(8,128)(2,1)} %copy-done), calls=%async_computation.2 | async-start | bytes 3145728 | tf_op jit(solution)/shard_map/all_to_all | solution.py:276
  159.8 1.2 copy-start.1
where the time goes:
time: 165 us
  waiting for transfers between devices  59.6 us (36%)
  Pallas kernels  40.5 us (25%)
  blocking collectives  40.5 us (25%)
  starting transfers between devices  16.9 us (10%)
  local copies, waits for them, and re-layouts  3.39 us (2%)
  other arithmetic  2.26 us (1%)
    all_to_all x1, waiting for transfers between devices, body(): exchanged = exchange(packed)  42.6 us
    all_to_all x1, blocking collectives, body(): stats = exchange(stats)  20.6 us
    all_gather x1, blocking collectives, body(): gain_terms = lax.all_gather(gain_part.reshape(-1), 'own')  20 us
    pallas_call x1, Pallas kernels, backward(): pl.pallas_call(backward_kernel, grid=(seq // QTILE,), out_shape=[jax.Shap...  19.8 us
    all_to_all x1, waiting for transfers between devices, body(): out_query, out_key, out_value = unpack(exchange(grads))  17 us
    pallas_call x1, Pallas kernels, forward(): pl.pallas_call(forward_kernel, grid=(seq // QTILE,), out_shape=[jax.Shape...  13.1 us
    all_to_all x1, starting transfers between devices, body(): exchanged = exchange(packed)  10.1 us
    pallas_call x1, Pallas kernels, pack(): pl.pallas_call(pack_kernel, grid=(steps,), out_shape=jax.ShapeDtypeStruct...  3.95 us
  transfers between devices with their start and end apart: 3, of which 2 were waited for; matrix products, arithmetic and copies ran while one was open for 2% of the time, Pallas kernels for 0%

commit v1 on v0

v1 whole, which is shorter than its diff:
```python
import functools
import math

import jax
import jax.numpy as jnp
from jax import lax
from jax.experimental import pallas as pl
from jax.experimental.pallas import tpu as pltpu
from jax.sharding import PartitionSpec as P

HDIM = 128
BLK = 64
WMAX = 2
PAIR = 2
GROUP = 8
NEG_FILL = -1e30
EPSILON = 1e-05
SCALE = 1.0 / math.sqrt(HDIM)
EXP_FACTOR = math.log2(math.e) * SCALE
VMEM_LIMIT = 40 * 1024 * 1024

NT = (((1,), (1,)), ((), ()))
TN = (((0,), (0,)), ((), ()))


def dot(a, b, dims=None):
    if dims is None:
        return jnp.dot(a, b, preferred_element_type=jnp.float32)
    return lax.dot_general(a, b, dims, preferred_element_type=jnp.float32)


def pack_kernel(q_ref, k_ref, v_ref, g_ref, out_ref, sems):
    heads = out_ref.shape[0]
    rows = q_ref.shape[1]
    copies = [
        pltpu.make_async_copy(
            ref.at[0, :, h * HDIM:(h + 1) * HDIM],
            out_ref.at[h, slot * rows:(slot + 1) * rows, :],
            sems.at[slot, h],
        )
        for slot, ref in enumerate((q_ref, k_ref, v_ref, g_ref))
        for h in range(heads)
    ]
    for copy in copies:
        copy.start()
    for copy in copies:
        copy.wait()


def pack(query_rows, key_rows, value_rows, out_grad):
    _, rows, cols = query_rows.shape
    heads = cols // HDIM
    return pl.pallas_call(
        pack_kernel,
        out_shape=jax.ShapeDtypeStruct((heads, 4 * rows, HDIM), query_rows.dtype),
        in_specs=[pl.BlockSpec(memory_space=pltpu.HBM)] * 4,
        out_specs=pl.BlockSpec(memory_space=pltpu.HBM),
        scratch_shapes=[pltpu.SemaphoreType.DMA((4, heads))],
        name="pack",
    )(query_rows, key_rows, value_rows, out_grad)


def unpack_kernel(in_ref, q_ref, k_ref, v_ref, sems):
    heads = in_ref.shape[0]
    rows = q_ref.shape[1]
    copies = [
        pltpu.make_async_copy(
            in_ref.at[h, slot * rows:(slot + 1) * rows, :],
            ref.at[0, :, h * HDIM:(h + 1) * HDIM],
            sems.at[slot, h],
        )
        for slot, ref in enumerate((q_ref, k_ref, v_ref))
        for h in range(heads)
    ]
    for copy in copies:
        copy.start()
    for copy in copies:
        copy.wait()


def unpack(exchanged):
    heads, rows3, _ = exchanged.shape
    rows = rows3 // 3
    shape = jax.ShapeDtypeStruct((1, rows, heads * HDIM), exchanged.dtype)
    return pl.pallas_call(
        unpack_kernel,
        out_shape=[shape] * 3,
        in_specs=[pl.BlockSpec(memory_space=pltpu.VMEM)],
        out_specs=[pl.BlockSpec(memory_space=pltpu.HBM)] * 3,
        scratch_shapes=[pltpu.SemaphoreType.DMA((3, heads))],
        name="unpack",
    )(exchanged)


def block_rows(ref, block, slot, rows):
    per = rows // BLK
    offset = pl.multiple_of(slot * rows + (block % per) * BLK, BLK)
    return ref[block // per, pl.ds(offset, BLK), :]


def all_rows(ref, slot, rows):
    return ref[:, slot * rows:(slot + 1) * rows, :].reshape(ref.shape[0] * rows, HDIM)


def forward_kernel(
    slots_ref, globs_ref, local_ref, in_ref, bias_ref, gain_ref,
    probs_ref, dense_ref, attn_ref, stat_ref,
    s_ref, sd_ref,
):
    devs, rows4, _ = in_ref.shape
    rows = rows4 // 4
    count = slots_ref.shape[1]
    globs = globs_ref.shape[0]
    width = count * BLK
    seq = devs * rows

    def gather(pair, slot):
        return jnp.concatenate(
            [block_rows(in_ref, slots_ref[pair, t], slot, rows) for t in range(count)], axis=0
        )

    def group(step, carry):
        pairs = [step * GROUP + u for u in range(GROUP)]
        tops = []
        for u, pair in enumerate(pairs):
            q = in_ref[pair, 0:rows, :]
            s = dot(q, gather(pair, 1), NT)
            s = jnp.concatenate(
                [s[b * BLK:(b + 1) * BLK] + bias_ref[pair, b:b + 1, :] for b in range(PAIR)], axis=0
            )
            s_ref[u] = s
            tops.append(jnp.max(s, axis=1, keepdims=True))
        sums = []
        for u, pair in enumerate(pairs):
            e = jnp.exp2((s_ref[u] - tops[u]) * EXP_FACTOR)
            s_ref[u] = e
            sums.append(jnp.sum(e, axis=1, keepdims=True))
        for u, pair in enumerate(pairs):
            row = lax.broadcasted_iota(jnp.int32, (rows, 1), 0)
            local = jnp.where(row < BLK, local_ref[pair, 0], local_ref[pair, 1])
            probs = (s_ref[u] * (local / sums[u])).astype(jnp.bfloat16)
            probs_ref[pair] = probs
            attn_ref[pair] = dot(probs, gather(pair, 2)).astype(jnp.bfloat16)
        return carry

    lax.fori_loop(0, devs // GROUP, group, 0)

    q = jnp.concatenate([block_rows(in_ref, globs_ref[t], 0, rows) for t in range(globs)], axis=0)
    step = 512
    tops = []
    for c in range(seq // step):
        keys = in_ref[c * 4:(c + 1) * 4, rows:2 * rows, :].reshape(step, HDIM)
        s = dot(q, keys, NT)
        sd_ref[:, c * step:(c + 1) * step] = s
        tops.append(jnp.max(s, axis=1, keepdims=True))
    top = functools.reduce(jnp.maximum, tops)
    total = jnp.zeros((globs * BLK, 1), jnp.float32)
    for c in range(seq // step):
        e = jnp.exp2((sd_ref[:, c * step:(c + 1) * step] - top) * EXP_FACTOR)
        sd_ref[:, c * step:(c + 1) * step] = e
        total = total + jnp.sum(e, axis=1, keepdims=True)
    inv = 1.0 / total
    for c in range(seq // step):
        dense_ref[:, c * step:(c + 1) * step] = (
            sd_ref[:, c * step:(c + 1) * step] * inv
        ).astype(jnp.bfloat16)
    out = dot(dense_ref[...], all_rows(in_ref, 2, rows)).astype(jnp.bfloat16)
    per = rows // BLK
    for t in range(globs):
        block = globs_ref[t]
        attn_ref[block // per, pl.ds(pl.multiple_of((block % per) * BLK, BLK), BLK), :] = (
            out[t * BLK:(t + 1) * BLK]
        )

    for i in range(devs):
        attn = attn_ref[i].astype(jnp.float32)
        grad = in_ref[i, 3 * rows:4 * rows, :].astype(jnp.float32) * gain_ref[...]
        square = jnp.sum((attn * attn).T, axis=0, keepdims=True)
        inner = jnp.sum((grad * attn).T, axis=0, keepdims=True)
        stats = jnp.concatenate([square, inner], axis=0)
        for d in range(devs):
            stat_ref[d, :, i * rows:(i + 1) * rows] = stats


def forward(slots, globs, local, exchanged, bias, gain_row):
    devs, rows4, _ = exchanged.shape
    rows = rows4 // 4
    seq = devs * rows
    width = slots.shape[1] * BLK
    smem = pl.BlockSpec(memory_space=pltpu.SMEM)
    vmem = pl.BlockSpec(memory_space=pltpu.VMEM)
    return pl.pallas_call(
        forward_kernel,
        out_shape=[
            jax.ShapeDtypeStruct((devs, rows, width), jnp.bfloat16),
            jax.ShapeDtypeStruct((globs.shape[0] * BLK, seq), jnp.bfloat16),
            jax.ShapeDtypeStruct((devs, rows, HDIM), jnp.bfloat16),
            jax.ShapeDtypeStruct((devs, 2, seq), jnp.float32),
        ],
        in_specs=[smem, smem, smem, vmem, vmem, vmem],
        out_specs=[vmem] * 4,
        scratch_shapes=[
            pltpu.VMEM((GROUP, rows, width), jnp.float32),
            pltpu.VMEM((globs.shape[0] * BLK, seq), jnp.float32),
        ],
        compiler_params=pltpu.CompilerParams(vmem_limit_bytes=VMEM_LIMIT),
        name="forward",
    )(slots, globs, local, exchanged, bias, gain_row)


def backward_kernel(
    slots_ref, globs_ref, in_ref, probs_ref, dense_ref, attn_ref, stat_ref, gain_ref,
    out_ref, gain_out_ref,
    low_ref, acc_ref, stage_ref, sem,
):
    devs, rows4, _ = in_ref.shape
    rows = rows4 // 4
    seq = devs * rows
    count = slots_ref.shape[1]
    globs = globs_ref.shape[0]

    stats = stat_ref[0]
    for d in range(1, devs):
        stats = stats + stat_ref[d]
    stats = stats * (1.0 / (devs * HDIM))
    inv_rms = lax.rsqrt(stats[0:1] + EPSILON)
    shrink = inv_rms * inv_rms * stats[1:2]
    gain = jnp.zeros((8, HDIM), jnp.float32)
    for i in range(devs):
        span = slice(i * rows, (i + 1) * rows)
        factor = jnp.broadcast_to(inv_rms[:, span], (HDIM, rows)).T
        minus = jnp.broadcast_to(shrink[:, span], (HDIM, rows)).T
        attn = attn_ref[i].astype(jnp.float32)
        grad = in_ref[i, 3 * rows:4 * rows, :].astype(jnp.float32)
        low_ref[i] = (factor * (gain_ref[...] * grad - attn * minus)).astype(jnp.bfloat16)
        gain = gain + jnp.sum((grad * attn * factor).reshape(rows // 8, 8, HDIM), axis=0)
    gain_out_ref[...] = jnp.sum(gain, axis=0, keepdims=True)

    def block_of(ref, block, slot):
        return block_rows(ref, block, slot, rows)

    def side(low, q):
        zero = jnp.zeros_like(low)
        return jnp.concatenate(
            [jnp.concatenate([low, zero], axis=1), jnp.concatenate([zero, q], axis=1)], axis=0
        )

    def row_dot(low, attn):
        return jnp.sum(low.astype(jnp.float32) * attn.astype(jnp.float32), axis=1, keepdims=True)

    blocks = [globs_ref[t] for t in range(globs)]
    q = jnp.concatenate([block_of(in_ref, b, 0) for b in blocks], axis=0)
    low = jnp.concatenate([block_of(low_ref, b, 0) for b in blocks], axis=0)
    attn = jnp.concatenate([block_of(attn_ref, b, 0) for b in blocks], axis=0)
    both = side(low, q)
    dots = row_dot(low, attn)
    step = 512
    dq_dense = jnp.zeros((globs * BLK, HDIM), jnp.float32)
    for c in range(seq // step):
        values = in_ref[c * 4:(c + 1) * 4, 2 * rows:3 * rows, :].reshape(step, HDIM)
        keys = in_ref[c * 4:(c + 1) * 4, rows:2 * rows, :].reshape(step, HDIM)
        probs = dense_ref[:, c * step:(c + 1) * step]
        ds = (probs.astype(jnp.float32) * (dot(low, values, NT) - dots)).astype(jnp.bfloat16)
        dq_dense = dq_dense + dot(ds, keys)
        acc_ref[c * step:(c + 1) * step, :] = dot(jnp.concatenate([probs, ds], axis=0), both, TN)

    def group(step, carry):
        results = []
        for u in range(GROUP):
            pair = step * GROUP + u
            ids = [slots_ref[pair, t] for t in range(count)]
            values = jnp.concatenate([block_of(in_ref, b, 2) for b in ids], axis=0)
            keys = jnp.concatenate([block_of(in_ref, b, 1) for b in ids], axis=0)
            q = in_ref[pair, 0:rows, :]
            low = low_ref[pair]
            probs = probs_ref[pair]
            dots = row_dot(low, attn_ref[pair])
            ds = (probs.astype(jnp.float32) * (dot(low, values, NT) - dots)).astype(jnp.bfloat16)
            stage_ref[pair, 0:rows, :] = (dot(ds, keys) * SCALE).astype(jnp.bfloat16)
            results.append((ids, dot(jnp.concatenate([probs, ds], axis=0), side(low, q), TN)))
        for ids, both in results:
            for t, block in enumerate(ids):
                acc_ref[pl.ds(pl.multiple_of(block * BLK, BLK), BLK), :] += (
                    both[t * BLK:(t + 1) * BLK]
                )
        return carry

    lax.fori_loop(0, devs // GROUP, group, 0)

    per = rows // BLK
    dq_dense = (dq_dense * SCALE).astype(jnp.bfloat16)
    for t, block in enumerate(blocks):
        stage_ref[block // per, pl.ds(pl.multiple_of((block % per) * BLK, BLK), BLK), :] = (
            dq_dense[t * BLK:(t + 1) * BLK]
        )
    for i in range(devs):
        span = slice(i * rows, (i + 1) * rows)
        stage_ref[i, rows:2 * rows, :] = (acc_ref[span, HDIM:] * SCALE).astype(jnp.bfloat16)
        stage_ref[i, 2 * rows:3 * rows, :] = acc_ref[span, :HDIM].astype(jnp.bfloat16)
    copy = pltpu.make_async_copy(stage_ref, out_ref, sem)
    copy.start()
    copy.wait()


def backward(slots, globs, exchanged, probs, dense, attn, stats, gain_row):
    devs, rows4, _ = exchanged.shape
    rows = rows4 // 4
    seq = devs * rows
    smem = pl.BlockSpec(memory_space=pltpu.SMEM)
    vmem = pl.BlockSpec(memory_space=pltpu.VMEM)
    return pl.pallas_call(
        backward_kernel,
        out_shape=[
            jax.ShapeDtypeStruct((devs, 3 * rows, HDIM), jnp.bfloat16),
            jax.ShapeDtypeStruct((1, HDIM), jnp.float32),
        ],
        in_specs=[smem, smem] + [vmem] * 6,
        out_specs=[pl.BlockSpec(memory_space=pltpu.HBM), vmem],
        scratch_shapes=[
            pltpu.VMEM((devs, rows, HDIM), jnp.bfloat16),
            pltpu.VMEM((seq, 2 * HDIM), jnp.float32),
            pltpu.VMEM((devs, 3 * rows, HDIM), jnp.bfloat16),
            pltpu.SemaphoreType.DMA,
        ],
        compiler_params=pltpu.CompilerParams(vmem_limit_bytes=VMEM_LIMIT),
        name="backward",
    )(slots, globs, exchanged, probs, dense, attn, stats, gain_row)


def pair_slots(head_width, filing_globals, head_random, count):
    pairs = count // PAIR
    first = jnp.arange(pairs, dtype=jnp.int32)[:, None] * PAIR
    near = first + jnp.arange(-WMAX, PAIR + WMAX, dtype=jnp.int32)[None, :]
    globs = jnp.broadcast_to(filing_globals[None, :], (pairs, filing_globals.shape[0]))
    rand = head_random.reshape(pairs, -1)
    ids = jnp.concatenate([near, globs, rand], axis=1)
    total = ids.shape[1]
    inside = (ids >= 0) & (ids < count)
    earlier = jnp.arange(total)[:, None] > jnp.arange(total)[None, :]
    again = jnp.any((ids[:, :, None] == ids[:, None, :]) & earlier[None], axis=2)
    live = inside & jnp.logical_not(again)
    queries = first + jnp.arange(PAIR, dtype=jnp.int32)[None, :]
    per_query = head_random.reshape(pairs, PAIR, 1, -1)
    keys = ids[:, None, :]
    allowed = (
        (jnp.abs(keys - queries[:, :, None]) <= head_width)
        | jnp.any(keys[..., None] == filing_globals, axis=-1)
        | jnp.any(keys[..., None] == per_query, axis=-1)
    )
    bias = jnp.where(allowed & live[:, None, :], 0.0, NEG_FILL).astype(jnp.float32)
    bias = jnp.repeat(bias, BLK, axis=2)
    is_global = jnp.any(queries[..., None] == filing_globals, axis=-1)
    local = jnp.where(is_global, 0.0, 1.0).astype(jnp.float32)
    return jnp.clip(ids, 0, count - 1), bias, local


def body(
    query_rows, key_rows, value_rows, out_grad, norm_gains, window, global_blocks, random_blocks
):
    seq_count = lax.axis_size("seq")
    own_count = lax.axis_size("own")
    rows = query_rows.shape[1]
    seq = rows * seq_count
    gain_scale = (own_count * seq) ** (-0.5)
    exchange = functools.partial(
        lax.all_to_all, axis_name="seq", split_axis=0, concat_axis=0, tiled=True
    )
    exchanged = exchange(pack(query_rows, key_rows, value_rows, out_grad))
    swap = [(o * own_count + s, s * own_count + o) for s in range(seq_count) for o in range(own_count)]
    gain_row = lax.ppermute(norm_gains, ("seq", "own"), swap).reshape(1, -1)
    globs = global_blocks[0]
    slots, bias, local = pair_slots(window[0], globs, random_blocks[0], seq // BLK)
    probs, dense, attn, stats = forward(slots, globs, local, exchanged, bias, gain_row)
    stats = exchange(stats)
    grads, gain_part = backward(slots, globs, exchanged, probs, dense, attn, stats, gain_row)
    gain_terms = lax.all_gather(gain_part.reshape(-1), "own")
    gain_grad = jnp.sum(gain_terms, axis=0) * gain_scale
    out_query, out_key, out_value = unpack(exchange(grads))
    return (out_query, out_key, out_value, gain_grad)


def solution(mesh):
    rows = P("own", "seq", None)
    placed = (rows, rows, rows, rows, P("own"), P("seq"), P("own", None), P("seq", None, None))
    return jax.shard_map(
        body,
        mesh=mesh,
        in_specs=placed,
        out_specs=(rows, rows, rows, P("seq")),
        check_vma=False,
    )
```

time: 165 us -> 208 us (1.26)
  Pallas kernels: 40.5 us -> 83.7 us
  waiting for transfers between devices: 59.6 us -> 63.6 us
  blocking collectives: 40.5 us -> 37.2 us
    pallas_call x4, Pallas kernels: 40.5 us -> 83.7 us  [the longest x1 65.2 us: pack(): pl.pallas_call(pack_kernel, out_shape=jax.ShapeDtypeStruct((heads, 4 * ro...]
    all_to_all x1, waiting for transfers between devices: 17 us -> 20.5 us  [body(): out_query, out_key, out_value = unpack(exchange(grads))]
    all_gather x1, blocking collectives: 20 us -> 16.8 us  [body(): gain_terms = lax.all_gather(gain_part.reshape(-1), 'own')]
  transfers between devices with their start and end apart: 3 -> 3, of which waited for: 2 -> 2; matrix products, arithmetic and copies ran while one was open for 2% -> 1% of each run, Pallas kernels for 0% -> 0%
where the time goes in v1:
time: 208 us
  Pallas kernels  83.7 us (40%)
  waiting for transfers between devices  63.6 us (31%)
  blocking collectives  37.2 us (18%)
  starting transfers between devices  16.9 us (8%)
  local copies, waits for them, and re-layouts  3.31 us (2%)
    pallas_call x1, Pallas kernels, pack(): pl.pallas_call(pack_kernel, out_shape=jax.ShapeDtypeStruct((heads, 4 * ro...  65.2 us
    all_to_all x1, waiting for transfers between devices, body(): exchanged = exchange(pack(query_rows, key_rows, value_rows, out_grad))  43.1 us
    all_to_all x1, waiting for transfers between devices, body(): out_query, out_key, out_value = unpack(exchange(grads))  20.5 us
    all_to_all x1, blocking collectives, body(): stats = exchange(stats)  20.5 us
    all_gather x1, blocking collectives, body(): gain_terms = lax.all_gather(gain_part.reshape(-1), 'own')  16.8 us
    all_to_all x1, starting transfers between devices, body(): exchanged = exchange(pack(query_rows, key_rows, value_rows, out_grad))  10.1 us
    pallas_call x1, Pallas kernels, backward(): pl.pallas_call(backward_kernel, out_shape=[jax.ShapeDtypeStruct((devs, 3...  8.15 us
    pallas_call x1, Pallas kernels, forward(): pl.pallas_call(forward_kernel, out_shape=[jax.ShapeDtypeStruct((devs, row...  7.35 us
  transfers between devices with their start and end apart: 3, of which 2 were waited for; matrix products, arithmetic and copies ran while one was open for 1% of the time, Pallas kernels for 0%

profile of v1, /device:TPU:1, one launch (start us, length us, event | category | flops | bytes accessed | tf_op | source)
XLA Modules:
  0.0 207.6 jit_solution(6435224199289478894)
XLA Ops:
  0.6 65.2 %pack.1 = bf16[16,512,128]{2,1,0:T(8,128)(2,1)} custom-call(bf16[1,128,2048]{2,1,0:T(8,128)(2,1)} %q_ref.1, bf16[1,128,2048]{2,1,0:T(8,128)(2,1)} %k_ref.1, bf16[1,128,2048]{2,1,0:T(8,128)(2,1)} %v_ref.1, bf16[1,128,2048]{2,1,0:T(8,128)(2,1)} %g_ref.1), custom_call_target="tpu_custom_call" | custom-call | tf_op jit(solution)/shard_map/pack/pallas_call | solution.py:53
  65.9 10.1 %all-to-all-start = ((bf16[16,512,128]{2,1,0:T(8,128)(2,1)}), bf16[16,512,128]{2,1,0:T(8,128)(2,1)S(1)}, u32[]{:S(2)}, u32[]{:S(2)}) async-start(bf16[16,512,128]{2,1,0:T(8,128)(2,1)} %pack.1), calls=%async_computation | async-start | bytes 4194304 | tf_op jit(solution)/shard_map/all_to_all | solution.py:368
  76.0 3.2 %collective-permute-start = (f32[128]{0:T(128)S(1)}, f32[128]{0:T(128)S(1)}, u32[]{:S(2)}, u32[]{:S(2)}) collective-permute-start(f32[128]{0:T(128)S(1)} %copy-done.4), channel_id=1, source_target_pairs={{0,0},{16,1},{32,2},{48,3},{64,4},{80,5},{96,6},{112,7},{128,8},{1... | collective-permute-start | bytes 1544 | tf_op jit(solution)/shard_map/ppermute | solution.py:370
  79.9 0.1 copy.22
  80.0 0.1 pad.1.clone
  80.1 0.1 compare_reduce_fusion.2
  80.2 0.1 copy.23
  80.3 0.1 reshape_squeeze.4
  80.3 0.1 broadcast_add_fusion
  80.4 0.1 broadcast_clamp_fusion
  80.5 0.1 copy.25
  80.6 0.4 and_reduce_fusion
  81.0 0.1 copy.26
  81.1 0.1 eq.69
  81.2 0.1 copy.24
  81.3 0.1 compare_reduce_fusion.1
  81.4 0.1 compare_reduce_fusion
  81.5 0.1 fusion.3
  81.6 0.1 broadcast_in_dim.44
  81.7 0.1 reshape.139
  81.8 0.1 copy.27.bias_ref
  81.9 43.1 %all-to-all-done.in_ref = bf16[16,512,128]{2,1,0:T(8,128)(2,1)S(1)} async-done(((bf16[16,512,128]{2,1,0:T(8,128)(2,1)}), bf16[16,512,128]{2,1,0:T(8,128)(2,1)S(1)}, u32[]{:S(2)}, u32[]{:S(2)}) %all-to-all-start) | async-done | bytes 2097184 | tf_op jit(solution)/shard_map/all_to_all | solution.py:368
  125.0 7.4 %forward.1 = (bf16[16,128,896]{2,1,0:T(8,128)(2,1)S(1)}, bf16[128,2048]{1,0:T(8,128)(2,1)S(1)}, bf16[16,128,128]{2,1,0:T(8,128)(2,1)S(1)}, f32[16,2,2048]{2,1,0:T(2,128)S(1)}) custom-call(s32[16,14]{1,0:T(8,128)S(1)} %get-tuple-element.22.slots_ref, s32[2]{0:T(128)S(1)} %bitcast.12, f32[16,2]{1,0:T(8,128)S(1)} %broadcast_select_fusion.local_ref, ...), custom_call_target="tpu_custom_call" | custom-call | tf_op jit(solution)/shard_map/forward/pallas_call | solution.py:192
  132.3 20.5 %all_to_all.15.stat_ref = f32[16,2,2048]{2,1,0:T(2,128)S(1)} all-to-all(f32[16,2,2048]{2,1,0:T(2,128)S(1)} %get-tuple-element.16), channel_id=1, replica_groups=mesh['seq'=16,'own'=16] {'seq'}, dimensions={0} | all-to-all | bytes 524288 | tf_op jit(solution)/shard_map/all_to_all | solution.py:374
  152.8 8.2 %backward.1 = (bf16[16,384,128]{2,1,0:T(8,128)(2,1)S(1)}, f32[1,128]{1,0:T(1,128)S(1)}) custom-call(s32[16,14]{1,0:T(8,128)S(1)} %get-tuple-element.22.slots_ref, s32[2]{0:T(128)S(1)} %bitcast.13, bf16[16,512,128]{2,1,0:T(8,128)(2,1)S(1)} %all-to-all-done.in_ref, bf16[16,128,896]{2,1,0:T(8,128)(2,1)S(1)} %get-tuple-element.13.probs_ref, ...), custom_call_target="tpu_custom_call" | custom-call | tf_op jit(solution)/shard_map/backward/pallas_call | solution.py:311
  160.9 1.1 copy-done
  162.1 3.6 %all-to-all-start.2 = ((bf16[16,384,128]{2,1,0:T(8,128)(2,1)}), bf16[16,384,128]{2,1,0:T(8,128)(2,1)S(1)}, u32[]{:S(2)}, u32[]{:S(2)}) async-start(bf16[16,384,128]{2,1,0:T(8,128)(2,1)} %copy-done), calls=%async_computation.2 | async-start | bytes 3145728 | tf_op jit(solution)/shard_map/all_to_all | solution.py:378
  165.7 16.8 %all-gather = f32[16,1,128]{2,1,0:T(1,128)S(1)} all-gather(f32[1,1,128]{2,1,0:T(1,128)S(1)} %bitcast.16), channel_id=1, replica_groups=mesh['seq'=16,'own'=16] {'own'}, dimensions={0}, use_global_device_ids=true | all-gather | bytes 8704 | tf_op jit(solution)/shard_map/all_gather | solution.py:376
  182.5 0.5 broadcast_multiply_fusion
  183.0 20.5 %all-to-all-done.2.in_ref = bf16[16,384,128]{2,1,0:T(8,128)(2,1)S(1)} async-done(((bf16[16,384,128]{2,1,0:T(8,128)(2,1)}), bf16[16,384,128]{2,1,0:T(8,128)(2,1)S(1)}, u32[]{:S(2)}, u32[]{:S(2)}) %all-to-all-start.2) | async-done | bytes 1572896 | tf_op jit(solution)/shard_map/all_to_all | solution.py:378
  203.5 1.2 copy-done.2
  204.7 2.9 %unpack.1 = (bf16[1,128,2048]{2,1,0:T(8,128)(2,1)}, bf16[1,128,2048]{2,1,0:T(8,128)(2,1)}, bf16[1,128,2048]{2,1,0:T(8,128)(2,1)}) custom-call(bf16[16,384,128]{2,1,0:T(8,128)(2,1)} %copy-done.2), custom_call_target="tpu_custom_call" | custom-call | tf_op jit(solution)/shard_map/unpack/pallas_call | solution.py:85
  (17 shorter events, 0.1 us)
Async XLA Ops:
  65.8 10.2 %copy-start.4 = (f32[128]{0:T(128)S(1)}, f32[128]{0:T(128)}, u32[]{:S(2)}) copy-start(f32[128]{0:T(128)} %param.12) | copy-start | bytes 1540
  65.9 14.0 %copy-start.3 = (s32[1,32,3]{1,0,2:T(1,128)S(1)}, s32[1,32,3]{1,0,2:T(1,128)}, u32[]{:S(2)}) copy-start(s32[1,32,3]{1,0,2:T(1,128)} %param.15) | copy-start | bytes 1156
  65.9 14.1 %copy-start.1 = (s32[1,2]{1,0:T(1,128)S(1)}, s32[1,2]{1,0:T(1,128)}, u32[]{:S(2)}) copy-start(s32[1,2]{1,0:T(1,128)} %param.14) | copy-start | bytes 28
  65.9 59.1 %all-to-all-start = ((bf16[16,512,128]{2,1,0:T(8,128)(2,1)}), bf16[16,512,128]{2,1,0:T(8,128)(2,1)S(1)}, u32[]{:S(2)}, u32[]{:S(2)}) async-start(bf16[16,512,128]{2,1,0:T(8,128)(2,1)} %pack.1), calls=%async_computation | async-start | bytes 4194304 | tf_op jit(solution)/shard_map/all_to_all | solution.py:368
  76.0 5.9 %collective-permute-start = (f32[128]{0:T(128)S(1)}, f32[128]{0:T(128)S(1)}, u32[]{:S(2)}, u32[]{:S(2)}) collective-permute-start(f32[128]{0:T(128)S(1)} %copy-done.4), channel_id=1, source_target_pairs={{0,0},{16,1},{32,2},{48,3},{64,4},{80,5},{96,6},{112,7},{128,8},{1... | collective-permute-start | bytes 1544 | tf_op jit(solution)/shard_map/ppermute | solution.py:370
  160.9 1.2 copy-start
  162.1 41.5 %all-to-all-start.2 = ((bf16[16,384,128]{2,1,0:T(8,128)(2,1)}), bf16[16,384,128]{2,1,0:T(8,128)(2,1)S(1)}, u32[]{:S(2)}, u32[]{:S(2)}) async-start(bf16[16,384,128]{2,1,0:T(8,128)(2,1)} %copy-done), calls=%async_computation.2 | async-start | bytes 3145728 | tf_op jit(solution)/shard_map/all_to_all | solution.py:378
  203.5 1.2 copy-start.2

commit v2 on v1

--- a/solution.py
+++ b/solution.py
@@ -18,6 +18,7 @@
 SCALE = 1.0 / math.sqrt(HDIM)
 EXP_FACTOR = math.log2(math.e) * SCALE
 VMEM_LIMIT = 40 * 1024 * 1024
+UNPACK_VMEM_LIMIT = 16 * 1024 * 1024
 
 NT = (((1,), (1,)), ((), ()))
 TN = (((0,), (0,)), ((), ()))
@@ -29,22 +30,32 @@
     return lax.dot_general(a, b, dims, preferred_element_type=jnp.float32)
 
 
-def pack_kernel(q_ref, k_ref, v_ref, g_ref, out_ref, sems):
+def pack_kernel(q_ref, k_ref, v_ref, g_ref, out_ref, stage_ref, in_sems, out_sems):
     heads = out_ref.shape[0]
     rows = q_ref.shape[1]
-    copies = [
-        pltpu.make_async_copy(
-            ref.at[0, :, h * HDIM:(h + 1) * HDIM],
-            out_ref.at[h, slot * rows:(slot + 1) * rows, :],
-            sems.at[slot, h],
-        )
-        for slot, ref in enumerate((q_ref, k_ref, v_ref, g_ref))
+    loads = [
+        [
+            pltpu.make_async_copy(
+                ref.at[0, :, h * HDIM:(h + 1) * HDIM],
+                stage_ref.at[h, slot * rows:(slot + 1) * rows, :],
+                in_sems.at[h, slot],
+            )
+            for slot, ref in enumerate((q_ref, k_ref, v_ref, g_ref))
+        ]
         for h in range(heads)
     ]
-    for copy in copies:
-        copy.start()
-    for copy in copies:
-        copy.wait()
+    stores = [
+        pltpu.make_async_copy(stage_ref.at[h], out_ref.at[h], out_sems.at[h]) for h in range(heads)
+    ]
+    for head_loads in loads:
+        for copy in head_loads:
+            copy.start()
+    for head_loads, store in zip(loads, stores):
+        for copy in head_loads:
+            copy.wait()
+        store.start()
+    for store in stores:
+        store.wait()
 
 
 def pack(query_rows, key_rows, value_rows, out_grad):
@@ -55,7 +66,11 @@
         out_shape=jax.ShapeDtypeStruct((heads, 4 * rows, HDIM), query_rows.dtype),
         in_specs=[pl.BlockSpec(memory_space=pltpu.HBM)] * 4,
         out_specs=pl.BlockSpec(memory_space=pltpu.HBM),
-        scratch_shapes=[pltpu.SemaphoreType.DMA((4, heads))],
+        scratch_shapes=[
+            pltpu.VMEM((heads, 4 * rows, HDIM), query_rows.dtype),
+            pltpu.SemaphoreType.DMA((heads, 4)),
+            pltpu.SemaphoreType.DMA((heads,)),
+        ],
         name="pack",
     )(query_rows, key_rows, value_rows, out_grad)
 
@@ -88,6 +103,7 @@
         in_specs=[pl.BlockSpec(memory_space=pltpu.VMEM)],
         out_specs=[pl.BlockSpec(memory_space=pltpu.HBM)] * 3,
         scratch_shapes=[pltpu.SemaphoreType.DMA((3, heads))],
+        compiler_params=pltpu.CompilerParams(vmem_limit_bytes=UNPACK_VMEM_LIMIT),
         name="unpack",
     )(exchanged)
 
@@ -311,7 +327,7 @@
     return pl.pallas_call(
         backward_kernel,
         out_shape=[
-            jax.ShapeDtypeStruct((devs, 3 * rows, HDIM), jnp.bfloat16),
+            pltpu.HBM((devs, 3 * rows, HDIM), jnp.bfloat16),
             jax.ShapeDtypeStruct((1, HDIM), jnp.float32),
         ],
         in_specs=[smem, smem] + [vmem] * 6,
@@ -366,8 +382,8 @@
         lax.all_to_all, axis_name="seq", split_axis=0, concat_axis=0, tiled=True
     )
     exchanged = exchange(pack(query_rows, key_rows, value_rows, out_grad))
-    swap = [(o * own_count + s, s * own_count + o) for s in range(seq_count) for o in range(own_count)]
-    gain_row = lax.ppermute(norm_gains, ("seq", "own"), swap).reshape(1, -1)
+    gains = lax.all_gather(norm_gains, "own")
+    gain_row = lax.dynamic_slice_in_dim(gains, lax.axis_index("seq"), 1, axis=0)
     globs = global_blocks[0]
     slots, bias, local = pair_slots(window[0], globs, random_blocks[0], seq // BLK)
     probs, dense, attn, stats = forward(slots, globs, local, exchanged, bias, gain_row)

time: 208 us -> 139 us (0.67)
  Pallas kernels: 83.7 us -> 21 us
  waiting for transfers between devices: 63.6 us -> 47.4 us
  blocking collectives: 37.2 us -> 52.6 us
  starting transfers between devices: 16.9 us -> 13.7 us
  local copies, waits for them, and re-layouts: 3.31 us -> 1.01 us
    pallas_call x1, Pallas kernels: 65.2 us -> 2.98 us  [pack(): pl.pallas_call(pack_kernel, out_shape=jax.ShapeDtypeStruct((heads, 4 * ro...]
    all_gather x0 -> x1, blocking collectives: none -> 18.1 us  [body(): gains = lax.all_gather(norm_gains, 'own')]
    all_to_all x1, waiting for transfers between devices: 43.1 us -> 28.2 us  [body(): exchanged = exchange(pack(query_rows, key_rows, value_rows, out_grad))]
    all_to_all x1, blocking collectives: 20.5 us -> 16.5 us  [body(): stats = exchange(stats)]
    ppermute x1 -> x0, starting transfers between devices: 3.19 us -> none  [body(): gain_row = lax.ppermute(norm_gains, ('seq', 'own'), swap).reshape(1, -1)]
    unnamed x11 -> x7, local copies, waits for them, and re-layouts: 2.41 us -> 0.11 us
  transfers between devices with their start and end apart: 3 -> 2, of which waited for: 2 -> 2; matrix products, arithmetic and copies ran while one was open for 1% -> 2% of each run, Pallas kernels for 0% -> 0%
where the time goes in v2:
time: 139 us
  blocking collectives  52.6 us (38%)
  waiting for transfers between devices  47.4 us (34%)
  Pallas kernels  21 us (15%)
  starting transfers between devices  13.7 us (10%)
  other arithmetic  1.5 us (1%)
  between operations  1.42 us (1%)
    all_to_all x1, waiting for transfers between devices, body(): exchanged = exchange(pack(query_rows, key_rows, value_rows, out_grad))  28.2 us
    all_to_all x1, waiting for transfers between devices, body(): out_query, out_key, out_value = unpack(exchange(grads))  19.2 us
    all_gather x1, blocking collectives, body(): gains = lax.all_gather(norm_gains, 'own')  18.1 us
    all_gather x1, blocking collectives, body(): gain_terms = lax.all_gather(gain_part.reshape(-1), 'own')  18.1 us
    all_to_all x1, blocking collectives, body(): stats = exchange(stats)  16.5 us
    all_to_all x1, starting transfers between devices, body(): exchanged = exchange(pack(query_rows, key_rows, value_rows, out_grad))  10.1 us
    pallas_call x1, Pallas kernels, backward(): pl.pallas_call(backward_kernel, out_shape=[pltpu.HBM((devs, 3 * rows, HDI...  9.12 us
    pallas_call x1, Pallas kernels, forward(): pl.pallas_call(forward_kernel, out_shape=[jax.ShapeDtypeStruct((devs, row...  7.35 us
  transfers between devices with their start and end apart: 2, of which 2 were waited for; matrix products, arithmetic and copies ran while one was open for 2% of the time, Pallas kernels for 0%

profile of v2, /device:TPU:1, one launch (start us, length us, event | category | flops | bytes accessed | tf_op | source)
XLA Modules:
  0.0 138.7 jit_solution(16795920962800544011)
XLA Ops:
  0.6 3.0 %pack.1 = bf16[16,512,128]{2,1,0:T(8,128)(2,1)} custom-call(bf16[1,128,2048]{2,1,0:T(8,128)(2,1)} %q_ref.1, bf16[1,128,2048]{2,1,0:T(8,128)(2,1)} %k_ref.1, bf16[1,128,2048]{2,1,0:T(8,128)(2,1)} %v_ref.1, bf16[1,128,2048]{2,1,0:T(8,128)(2,1)} %g_ref.1), custom_call_target="tpu_custom_call" | custom-call | tf_op jit(solution)/shard_map/pack/pallas_call | solution.py:64
  3.6 0.0 copy-start
  3.6 0.0 copy-start.2
  3.7 10.1 %all-to-all-start = ((bf16[16,512,128]{2,1,0:T(8,128)(2,1)}), bf16[16,512,128]{2,1,0:T(8,128)(2,1)S(1)}, u32[]{:S(2)}, u32[]{:S(2)}) async-start(bf16[16,512,128]{2,1,0:T(8,128)(2,1)} %pack.1), calls=%async_computation | async-start | bytes 4194304 | tf_op jit(solution)/shard_map/all_to_all | solution.py:384
  13.8 0.1 copy.22
  14.6 0.1 pad.1.clone
  14.6 0.1 compare_reduce_fusion.2
  14.7 0.1 copy.23
  14.8 0.1 reshape_squeeze.4
  14.9 0.1 broadcast_add_fusion
  15.0 0.1 broadcast_clamp_fusion
  15.1 0.1 copy.25
  15.2 0.4 and_reduce_fusion
  15.6 0.1 copy.26
  15.7 0.1 eq.69
  15.8 0.1 copy.24
  15.9 0.1 compare_reduce_fusion.1
  15.9 0.1 compare_reduce_fusion
  16.0 0.1 fusion.3
  16.1 0.1 broadcast_in_dim.44
  16.3 0.1 reshape.136
  16.4 0.1 copy.27.bias_ref
  16.5 18.1 %all-gather.1 = f32[16,1,128]{2,1,0:T(1,128)S(1)} all-gather(f32[1,1,128]{2,1,0:T(1,128)S(1)} %bitcast.17), channel_id=2, replica_groups=mesh['seq'=16,'own'=16] {'own'}, dimensions={0}, use_global_device_ids=true | all-gather | bytes 8704 | tf_op jit(solution)/shard_map/all_gather | solution.py:385
  34.6 28.2 %all-to-all-done.in_ref = bf16[16,512,128]{2,1,0:T(8,128)(2,1)S(1)} async-done(((bf16[16,512,128]{2,1,0:T(8,128)(2,1)}), bf16[16,512,128]{2,1,0:T(8,128)(2,1)S(1)}, u32[]{:S(2)}, u32[]{:S(2)}) %all-to-all-start) | async-done | bytes 2097184 | tf_op jit(solution)/shard_map/all_to_all | solution.py:384
  62.7 7.4 %forward.1 = (bf16[16,128,896]{2,1,0:T(8,128)(2,1)S(1)}, bf16[128,2048]{1,0:T(8,128)(2,1)S(1)}, bf16[16,128,128]{2,1,0:T(8,128)(2,1)S(1)}, f32[16,2,2048]{2,1,0:T(2,128)S(1)}) custom-call(s32[16,14]{1,0:T(8,128)S(1)} %get-tuple-element.22.slots_ref, s32[2]{0:T(128)S(1)} %bitcast.14, f32[16,2]{1,0:T(8,128)S(1)} %broadcast_select_fusion.local_ref, ...), custom_call_target="tpu_custom_call" | custom-call | tf_op jit(solution)/shard_map/forward/pallas_call | solution.py:208
  70.1 16.5 %all_to_all.15.stat_ref = f32[16,2,2048]{2,1,0:T(2,128)S(1)} all-to-all(f32[16,2,2048]{2,1,0:T(2,128)S(1)} %get-tuple-element.16), channel_id=1, replica_groups=mesh['seq'=16,'own'=16] {'seq'}, dimensions={0} | all-to-all | bytes 524288 | tf_op jit(solution)/shard_map/all_to_all | solution.py:390
  86.6 9.1 %backward.1 = (bf16[16,384,128]{2,1,0:T(8,128)(2,1)}, f32[1,128]{1,0:T(1,128)S(1)}) custom-call(s32[16,14]{1,0:T(8,128)S(1)} %get-tuple-element.22.slots_ref, s32[2]{0:T(128)S(1)} %bitcast.15, bf16[16,512,128]{2,1,0:T(8,128)(2,1)S(1)} %all-to-all-done.in_ref, bf16[16,128,896]{2,1,0:T(8,128)(2,1)S(1)} %get-tuple-element.13.probs_ref, ...), custom_call_target="tpu_custom_call" | custom-call | tf_op jit(solution)/shard_map/backward/pallas_call | solution.py:327
  95.7 3.6 %all-to-all-start.2 = ((bf16[16,384,128]{2,1,0:T(8,128)(2,1)}), bf16[16,384,128]{2,1,0:T(8,128)(2,1)S(1)}, u32[]{:S(2)}, u32[]{:S(2)}) async-start(bf16[16,384,128]{2,1,0:T(8,128)(2,1)} %get-tuple-element.17), calls=%async_computation.2 | async-start | bytes 3145728 | tf_op jit(solution)/shard_map/all_to_all | solution.py:394
  99.3 18.1 %all-gather.2 = f32[16,1,128]{2,1,0:T(1,128)S(1)} all-gather(f32[1,1,128]{2,1,0:T(1,128)S(1)} %bitcast.16), channel_id=1, replica_groups=mesh['seq'=16,'own'=16] {'own'}, dimensions={0}, use_global_device_ids=true | all-gather | bytes 8704 | tf_op jit(solution)/shard_map/all_gather | solution.py:392
  117.4 0.5 broadcast_multiply_fusion
  118.0 19.2 %all-to-all-done.2.in_ref = bf16[16,384,128]{2,1,0:T(8,128)(2,1)S(1)} async-done(((bf16[16,384,128]{2,1,0:T(8,128)(2,1)}), bf16[16,384,128]{2,1,0:T(8,128)(2,1)S(1)}, u32[]{:S(2)}, u32[]{:S(2)}) %all-to-all-start.2) | async-done | bytes 1572896 | tf_op jit(solution)/shard_map/all_to_all | solution.py:394
  137.2 1.5 %unpack.1 = (bf16[1,128,2048]{2,1,0:T(8,128)(2,1)}, bf16[1,128,2048]{2,1,0:T(8,128)(2,1)}, bf16[1,128,2048]{2,1,0:T(8,128)(2,1)}) custom-call(bf16[16,384,128]{2,1,0:T(8,128)(2,1)S(1)} %all-to-all-done.2.in_ref), custom_call_target="tpu_custom_call" | custom-call | tf_op jit(solution)/shard_map/unpack/pallas_call | solution.py:100
  (13 shorter events, 0.1 us)
Async XLA Ops:
  3.6 10.2 %copy-start.1 = (s32[1,32,3]{1,0,2:T(1,128)S(1)}, s32[1,32,3]{1,0,2:T(1,128)}, u32[]{:S(2)}) copy-start(s32[1,32,3]{1,0,2:T(1,128)} %param.15) | copy-start | bytes 1156
  3.6 10.9 %copy-start = (s32[1,2]{1,0:T(1,128)S(1)}, s32[1,2]{1,0:T(1,128)}, u32[]{:S(2)}) copy-start(s32[1,2]{1,0:T(1,128)} %param.14) | copy-start | bytes 28
  3.6 12.8 %copy-start.2 = (f32[128]{0:T(128)S(1)}, f32[128]{0:T(128)}, u32[]{:S(2)}) copy-start(f32[128]{0:T(128)} %param.12) | copy-start | bytes 1540
  3.7 59.1 %all-to-all-start = ((bf16[16,512,128]{2,1,0:T(8,128)(2,1)}), bf16[16,512,128]{2,1,0:T(8,128)(2,1)S(1)}, u32[]{:S(2)}, u32[]{:S(2)}) async-start(bf16[16,512,128]{2,1,0:T(8,128)(2,1)} %pack.1), calls=%async_computation | async-start | bytes 4194304 | tf_op jit(solution)/shard_map/all_to_all | solution.py:384
  95.7 41.5 %all-to-all-start.2 = ((bf16[16,384,128]{2,1,0:T(8,128)(2,1)}), bf16[16,384,128]{2,1,0:T(8,128)(2,1)S(1)}, u32[]{:S(2)}, u32[]{:S(2)}) async-start(bf16[16,384,128]{2,1,0:T(8,128)(2,1)} %get-tuple-element.17), calls=%async_computation.2 | async-start | bytes 3145728 | tf_op jit(solution)/shard_map/all_to_all | solution.py:394

commit v3 on v2

--- a/solution.py
+++ b/solution.py
@@ -12,12 +12,16 @@
 BLK = 64
 WMAX = 2
 PAIR = 2
-GROUP = 8
+GLOB = 2
+GLOB_AT = PAIR + 2 * WMAX
+GROUP = 16
 NEG_FILL = -1e30
 EPSILON = 1e-05
 SCALE = 1.0 / math.sqrt(HDIM)
 EXP_FACTOR = math.log2(math.e) * SCALE
 VMEM_LIMIT = 40 * 1024 * 1024
+SUM_LOW = 2.0 ** -80
+SUM_HIGH = 2.0 ** 80
 UNPACK_VMEM_LIMIT = 16 * 1024 * 1024
 
 NT = (((1,), (1,)), ((), ()))
@@ -119,74 +123,108 @@
 
 
 def forward_kernel(
-    slots_ref, globs_ref, local_ref, in_ref, bias_ref, gain_ref,
-    probs_ref, dense_ref, attn_ref, stat_ref,
-    s_ref, sd_ref,
+    slots_ref, in_ref, bias_ref, gain_ref,
+    probs_ref, dense_ref, attn_ref, inv_ref, inv_dense_ref, stat_ref,
+    low_ref, high_ref,
 ):
     devs, rows4, _ = in_ref.shape
     rows = rows4 // 4
     count = slots_ref.shape[1]
-    globs = globs_ref.shape[0]
-    width = count * BLK
-    seq = devs * rows
+    globs = GLOB
+    glob_ids = [slots_ref[0, GLOB_AT + t] for t in range(globs)]
+    per = rows // BLK
 
     def gather(pair, slot):
         return jnp.concatenate(
             [block_rows(in_ref, slots_ref[pair, t], slot, rows) for t in range(count)], axis=0
         )
 
+    def pair_pass(pair, exact):
+        s = dot(in_ref[pair, 0:rows, :], gather(pair, 1), NT)
+        bias = bias_ref[pair]
+        if exact:
+            s = jnp.concatenate(
+                [s[b * BLK:(b + 1) * BLK] + bias[b:b + 1] for b in range(PAIR)], axis=0
+            )
+            e = jnp.exp2((s - jnp.max(s, axis=1, keepdims=True)) * EXP_FACTOR)
+        else:
+            e = jnp.concatenate(
+                [
+                    jnp.exp2(s[b * BLK:(b + 1) * BLK] * EXP_FACTOR + bias[b:b + 1])
+                    for b in range(PAIR)
+                ],
+                axis=0,
+            )
+        e = e.astype(jnp.bfloat16)
+        values = jnp.concatenate(
+            [gather(pair, 2), jnp.ones((count * BLK, HDIM), jnp.bfloat16)], axis=1
+        )
+        out = dot(e, values)
+        total = out[:, HDIM:]
+        row = lax.broadcasted_iota(jnp.int32, (rows, HDIM), 0)
+        local = []
+        for b in range(PAIR):
+            is_global = functools.reduce(
+                jnp.logical_or, [pair * PAIR + b == block for block in glob_ids]
+            )
+            local.append(jnp.where(is_global, 0.0, 1.0))
+        inv = jnp.where(row < BLK, local[0], local[1]) / total
+        probs_ref[pair] = e
+        inv_ref[pair] = inv
+        attn_ref[pair] = (out[:, :HDIM] * inv).astype(jnp.bfloat16)
+        return total
+
+    def dense_pass(exact):
+        q = jnp.concatenate(
+            [block_rows(in_ref, block, 0, rows) for block in glob_ids], axis=0
+        )
+        if exact:
+            top = jnp.full((globs * BLK, 1), NEG_FILL, jnp.float32)
+            for c in range(devs):
+                s = dot(q, in_ref[c, rows:2 * rows, :], NT)
+                top = jnp.maximum(top, jnp.max(s, axis=1, keepdims=True))
+        else:
+            top = 0.0
+        out = jnp.zeros((globs * BLK, 2 * HDIM), jnp.float32)
+        ones = jnp.ones((2 * rows, HDIM), jnp.bfloat16)
+        for c in range(devs // 2):
+            keys = in_ref[2 * c:2 * c + 2, rows:2 * rows, :].reshape(2 * rows, HDIM)
+            values = in_ref[2 * c:2 * c + 2, 2 * rows:3 * rows, :].reshape(2 * rows, HDIM)
+            e = jnp.exp2((dot(q, keys, NT) - top) * EXP_FACTOR).astype(jnp.bfloat16)
+            dense_ref[:, 2 * c * rows:2 * (c + 1) * rows] = e
+            out = out + dot(e, jnp.concatenate([values, ones], axis=1))
+        total = out[:, HDIM:]
+        inv = 1.0 / total
+        inv_dense_ref[...] = inv
+        out = (out[:, :HDIM] * inv).astype(jnp.bfloat16)
+        for t, block in enumerate(glob_ids):
+            attn_ref[block // per, pl.ds(pl.multiple_of((block % per) * BLK, BLK), BLK), :] = (
+                out[t * BLK:(t + 1) * BLK]
+            )
+        return total
+
     def group(step, carry):
-        pairs = [step * GROUP + u for u in range(GROUP)]
-        tops = []
-        for u, pair in enumerate(pairs):
-            q = in_ref[pair, 0:rows, :]
-            s = dot(q, gather(pair, 1), NT)
-            s = jnp.concatenate(
-                [s[b * BLK:(b + 1) * BLK] + bias_ref[pair, b:b + 1, :] for b in range(PAIR)], axis=0
-            )
-            s_ref[u] = s
-            tops.append(jnp.max(s, axis=1, keepdims=True))
-        sums = []
-        for u, pair in enumerate(pairs):
-            e = jnp.exp2((s_ref[u] - tops[u]) * EXP_FACTOR)
-            s_ref[u] = e
-            sums.append(jnp.sum(e, axis=1, keepdims=True))
-        for u, pair in enumerate(pairs):
-            row = lax.broadcasted_iota(jnp.int32, (rows, 1), 0)
-            local = jnp.where(row < BLK, local_ref[pair, 0], local_ref[pair, 1])
-            probs = (s_ref[u] * (local / sums[u])).astype(jnp.bfloat16)
-            probs_ref[pair] = probs
-            attn_ref[pair] = dot(probs, gather(pair, 2)).astype(jnp.bfloat16)
+        totals = [pair_pass(step * GROUP + u, False) for u in range(GROUP)]
+        low_ref[...] = functools.reduce(jnp.minimum, totals, low_ref[...])
+        high_ref[...] = functools.reduce(jnp.maximum, totals, high_ref[...])
         return carry
 
+    def single(pair, carry):
+        pair_pass(pair, True)
+        return carry
+
+    low_ref[...] = jnp.full_like(low_ref, 1.0)
+    high_ref[...] = jnp.full_like(high_ref, 1.0)
     lax.fori_loop(0, devs // GROUP, group, 0)
-
-    q = jnp.concatenate([block_rows(in_ref, globs_ref[t], 0, rows) for t in range(globs)], axis=0)
-    step = 512
-    tops = []
-    for c in range(seq // step):
-        keys = in_ref[c * 4:(c + 1) * 4, rows:2 * rows, :].reshape(step, HDIM)
-        s = dot(q, keys, NT)
-        sd_ref[:, c * step:(c + 1) * step] = s
-        tops.append(jnp.max(s, axis=1, keepdims=True))
-    top = functools.reduce(jnp.maximum, tops)
-    total = jnp.zeros((globs * BLK, 1), jnp.float32)
-    for c in range(seq // step):
-        e = jnp.exp2((sd_ref[:, c * step:(c + 1) * step] - top) * EXP_FACTOR)
-        sd_ref[:, c * step:(c + 1) * step] = e
-        total = total + jnp.sum(e, axis=1, keepdims=True)
-    inv = 1.0 / total
-    for c in range(seq // step):
-        dense_ref[:, c * step:(c + 1) * step] = (
-            sd_ref[:, c * step:(c + 1) * step] * inv
-        ).astype(jnp.bfloat16)
-    out = dot(dense_ref[...], all_rows(in_ref, 2, rows)).astype(jnp.bfloat16)
-    per = rows // BLK
-    for t in range(globs):
-        block = globs_ref[t]
-        attn_ref[block // per, pl.ds(pl.multiple_of((block % per) * BLK, BLK), BLK), :] = (
-            out[t * BLK:(t + 1) * BLK]
-        )
+    total = dense_pass(False)
+    low = jnp.min(jnp.minimum(low_ref[...], total))
+    high = jnp.max(jnp.maximum(high_ref[...], total))
+    in_range = (low > SUM_LOW) & (high < SUM_HIGH)
+
+    @pl.when(jnp.logical_not(in_range))
+    def _():
+        lax.fori_loop(0, devs, single, 0)
+        dense_pass(True)
 
     for i in range(devs):
         attn = attn_ref[i].astype(jnp.float32)
@@ -198,7 +236,7 @@
             stat_ref[d, :, i * rows:(i + 1) * rows] = stats
 
 
-def forward(slots, globs, local, exchanged, bias, gain_row):
+def forward(slots, exchanged, bias, gain_row):
     devs, rows4, _ = exchanged.shape
     rows = rows4 // 4
     seq = devs * rows
@@ -209,31 +247,31 @@
         forward_kernel,
         out_shape=[
             jax.ShapeDtypeStruct((devs, rows, width), jnp.bfloat16),
-            jax.ShapeDtypeStruct((globs.shape[0] * BLK, seq), jnp.bfloat16),
+            jax.ShapeDtypeStruct((GLOB * BLK, seq), jnp.bfloat16),
             jax.ShapeDtypeStruct((devs, rows, HDIM), jnp.bfloat16),
+            jax.ShapeDtypeStruct((devs, rows, HDIM), jnp.float32),
+            jax.ShapeDtypeStruct((GLOB * BLK, HDIM), jnp.float32),
             jax.ShapeDtypeStruct((devs, 2, seq), jnp.float32),
         ],
-        in_specs=[smem, smem, smem, vmem, vmem, vmem],
-        out_specs=[vmem] * 4,
-        scratch_shapes=[
-            pltpu.VMEM((GROUP, rows, width), jnp.float32),
-            pltpu.VMEM((globs.shape[0] * BLK, seq), jnp.float32),
-        ],
+        in_specs=[smem, vmem, vmem, vmem],
+        out_specs=[vmem] * 6,
+        scratch_shapes=[pltpu.VMEM((rows, HDIM), jnp.float32)] * 2,
         compiler_params=pltpu.CompilerParams(vmem_limit_bytes=VMEM_LIMIT),
         name="forward",
-    )(slots, globs, local, exchanged, bias, gain_row)
+    )(slots, exchanged, bias, gain_row)
 
 
 def backward_kernel(
-    slots_ref, globs_ref, in_ref, probs_ref, dense_ref, attn_ref, stat_ref, gain_ref,
+    slots_ref, in_ref, probs_ref, dense_ref, attn_ref, inv_ref, inv_dense_ref, stat_ref,
+    gain_ref,
     out_ref, gain_out_ref,
-    low_ref, acc_ref, stage_ref, sem,
+    grad_ref, acc_ref, stage_ref, sems,
 ):
     devs, rows4, _ = in_ref.shape
     rows = rows4 // 4
     seq = devs * rows
     count = slots_ref.shape[1]
-    globs = globs_ref.shape[0]
+    globs = GLOB
 
     stats = stat_ref[0]
     for d in range(1, devs):
@@ -248,7 +286,7 @@
         minus = jnp.broadcast_to(shrink[:, span], (HDIM, rows)).T
         attn = attn_ref[i].astype(jnp.float32)
         grad = in_ref[i, 3 * rows:4 * rows, :].astype(jnp.float32)
-        low_ref[i] = (factor * (gain_ref[...] * grad - attn * minus)).astype(jnp.bfloat16)
+        grad_ref[i] = factor * (gain_ref[...] * grad - attn * minus)
         gain = gain + jnp.sum((grad * attn * factor).reshape(rows // 8, 8, HDIM), axis=0)
     gain_out_ref[...] = jnp.sum(gain, axis=0, keepdims=True)
 
@@ -264,9 +302,10 @@
     def row_dot(low, attn):
         return jnp.sum(low.astype(jnp.float32) * attn.astype(jnp.float32), axis=1, keepdims=True)
 
-    blocks = [globs_ref[t] for t in range(globs)]
+    blocks = [slots_ref[0, GLOB_AT + t] for t in range(globs)]
     q = jnp.concatenate([block_of(in_ref, b, 0) for b in blocks], axis=0)
-    low = jnp.concatenate([block_of(low_ref, b, 0) for b in blocks], axis=0)
+    low = jnp.concatenate([block_of(grad_ref, b, 0) for b in blocks], axis=0) * inv_dense_ref[...]
+    low = low.astype(jnp.bfloat16)
     attn = jnp.concatenate([block_of(attn_ref, b, 0) for b in blocks], axis=0)
     both = side(low, q)
     dots = row_dot(low, attn)
@@ -281,20 +320,18 @@
         acc_ref[c * step:(c + 1) * step, :] = dot(jnp.concatenate([probs, ds], axis=0), both, TN)
 
     def group(step, carry):
-        results = []
         for u in range(GROUP):
             pair = step * GROUP + u
             ids = [slots_ref[pair, t] for t in range(count)]
             values = jnp.concatenate([block_of(in_ref, b, 2) for b in ids], axis=0)
             keys = jnp.concatenate([block_of(in_ref, b, 1) for b in ids], axis=0)
             q = in_ref[pair, 0:rows, :]
-            low = low_ref[pair]
+            low = (grad_ref[pair] * inv_ref[pair]).astype(jnp.bfloat16)
             probs = probs_ref[pair]
             dots = row_dot(low, attn_ref[pair])
             ds = (probs.astype(jnp.float32) * (dot(low, values, NT) - dots)).astype(jnp.bfloat16)
             stage_ref[pair, 0:rows, :] = (dot(ds, keys) * SCALE).astype(jnp.bfloat16)
-            results.append((ids, dot(jnp.concatenate([probs, ds], axis=0), side(low, q), TN)))
-        for ids, both in results:
+            both = dot(jnp.concatenate([probs, ds], axis=0), side(low, q), TN)
             for t, block in enumerate(ids):
                 acc_ref[pl.ds(pl.multiple_of(block * BLK, BLK), BLK), :] += (
                     both[t * BLK:(t + 1) * BLK]
@@ -309,16 +346,18 @@
         stage_ref[block // per, pl.ds(pl.multiple_of((block % per) * BLK, BLK), BLK), :] = (
             dq_dense[t * BLK:(t + 1) * BLK]
         )
+    copies = []
     for i in range(devs):
         span = slice(i * rows, (i + 1) * rows)
         stage_ref[i, rows:2 * rows, :] = (acc_ref[span, HDIM:] * SCALE).astype(jnp.bfloat16)
         stage_ref[i, 2 * rows:3 * rows, :] = acc_ref[span, :HDIM].astype(jnp.bfloat16)
-    copy = pltpu.make_async_copy(stage_ref, out_ref, sem)
-    copy.start()
-    copy.wait()
-
-
-def backward(slots, globs, exchanged, probs, dense, attn, stats, gain_row):
+        copies.append(pltpu.make_async_copy(stage_ref.at[i], out_ref.at[i], sems.at[i]))
+        copies[-1].start()
+    for copy in copies:
+        copy.wait()
+
+
+def backward(slots, exchanged, forwarded, stats, gain_row):
     devs, rows4, _ = exchanged.shape
     rows = rows4 // 4
     seq = devs * rows
@@ -330,17 +369,17 @@
             pltpu.HBM((devs, 3 * rows, HDIM), jnp.bfloat16),
             jax.ShapeDtypeStruct((1, HDIM), jnp.float32),
         ],
-        in_specs=[smem, smem] + [vmem] * 6,
+        in_specs=[smem] + [vmem] * 8,
         out_specs=[pl.BlockSpec(memory_space=pltpu.HBM), vmem],
         scratch_shapes=[
-            pltpu.VMEM((devs, rows, HDIM), jnp.bfloat16),
+            pltpu.VMEM((devs, rows, HDIM), jnp.float32),
             pltpu.VMEM((seq, 2 * HDIM), jnp.float32),
             pltpu.VMEM((devs, 3 * rows, HDIM), jnp.bfloat16),
-            pltpu.SemaphoreType.DMA,
+            pltpu.SemaphoreType.DMA((devs,)),
         ],
         compiler_params=pltpu.CompilerParams(vmem_limit_bytes=VMEM_LIMIT),
         name="backward",
-    )(slots, globs, exchanged, probs, dense, attn, stats, gain_row)
+    )(slots, exchanged, *forwarded, stats, gain_row)
 
 
 def pair_slots(head_width, filing_globals, head_random, count):
@@ -365,9 +404,7 @@
     )
     bias = jnp.where(allowed & live[:, None, :], 0.0, NEG_FILL).astype(jnp.float32)
     bias = jnp.repeat(bias, BLK, axis=2)
-    is_global = jnp.any(queries[..., None] == filing_globals, axis=-1)
-    local = jnp.where(is_global, 0.0, 1.0).astype(jnp.float32)
-    return jnp.clip(ids, 0, count - 1), bias, local
+    return jnp.clip(ids, 0, count - 1), bias
 
 
 def body(
@@ -384,11 +421,10 @@
     exchanged = exchange(pack(query_rows, key_rows, value_rows, out_grad))
     gains = lax.all_gather(norm_gains, "own")
     gain_row = lax.dynamic_slice_in_dim(gains, lax.axis_index("seq"), 1, axis=0)
-    globs = global_blocks[0]
-    slots, bias, local = pair_slots(window[0], globs, random_blocks[0], seq // BLK)
-    probs, dense, attn, stats = forward(slots, globs, local, exchanged, bias, gain_row)
+    slots, bias = pair_slots(window[0], global_blocks[0], random_blocks[0], seq // BLK)
+    *forwarded, stats = forward(slots, exchanged, bias, gain_row)
     stats = exchange(stats)
-    grads, gain_part = backward(slots, globs, exchanged, probs, dense, attn, stats, gain_row)
+    grads, gain_part = backward(slots, exchanged, forwarded, stats, gain_row)
     gain_terms = lax.all_gather(gain_part.reshape(-1), "own")
     gain_grad = jnp.sum(gain_terms, axis=0) * gain_scale
     out_query, out_key, out_value = unpack(exchange(grads))

time: 139 us -> 146 us (1.050)
  Pallas kernels: 21 us -> 28.2 us
    pallas_call x1, Pallas kernels: 7.35 us -> 15.6 us  [forward(): pl.pallas_call(forward_kernel, out_shape=[jax.ShapeDtypeStruct((devs, row...]
where the time goes in v3:
time: 146 us
  blocking collectives  52.6 us (36%)
  waiting for transfers between devices  47.6 us (33%)
  Pallas kernels  28.2 us (19%)
  starting transfers between devices  13.7 us (9%)
  between operations  1.58 us (1%)
    all_to_all x1, waiting for transfers between devices, body(): exchanged = exchange(pack(query_rows, key_rows, value_rows, out_grad))  28.4 us
    all_to_all x1, waiting for transfers between devices, body(): out_query, out_key, out_value = unpack(exchange(grads))  19.2 us
    all_gather x1, blocking collectives, body(): gains = lax.all_gather(norm_gains, 'own')  18.1 us
    all_gather x1, blocking collectives, body(): gain_terms = lax.all_gather(gain_part.reshape(-1), 'own')  18.1 us
    all_to_all x1, blocking collectives, body(): stats = exchange(stats)  16.5 us
    pallas_call x1, Pallas kernels, forward(): pl.pallas_call(forward_kernel, out_shape=[jax.ShapeDtypeStruct((devs, row...  15.6 us
    all_to_all x1, starting transfers between devices, body(): exchanged = exchange(pack(query_rows, key_rows, value_rows, out_grad))  10.1 us
    pallas_call x1, Pallas kernels, backward(): pl.pallas_call(backward_kernel, out_shape=[pltpu.HBM((devs, 3 * rows, HDI...  8.05 us
  transfers between devices with their start and end apart: 2, of which 2 were waited for; matrix products, arithmetic and copies ran while one was open for 2% of the time, Pallas kernels for 0%

profile of v3, /device:TPU:1, one launch (start us, length us, event | category | flops | bytes accessed | tf_op | source)
XLA Modules:
  0.0 146.1 jit_solution(4143401934979516842)
XLA Ops:
  0.6 3.0 %pack.1 = bf16[16,512,128]{2,1,0:T(8,128)(2,1)} custom-call(bf16[1,128,2048]{2,1,0:T(8,128)(2,1)} %q_ref.1, bf16[1,128,2048]{2,1,0:T(8,128)(2,1)} %k_ref.1, bf16[1,128,2048]{2,1,0:T(8,128)(2,1)} %v_ref.1, bf16[1,128,2048]{2,1,0:T(8,128)(2,1)} %g_ref.1), custom_call_target="tpu_custom_call" | custom-call | tf_op jit(solution)/shard_map/pack/pallas_call | solution.py:68
  3.6 0.0 copy-start
  3.6 0.0 copy-start.2
  3.6 0.0 copy-start.1
  3.7 10.1 %all-to-all-start = ((bf16[16,512,128]{2,1,0:T(8,128)(2,1)}), bf16[16,512,128]{2,1,0:T(8,128)(2,1)S(1)}, u32[]{:S(2)}, u32[]{:S(2)}) async-start(bf16[16,512,128]{2,1,0:T(8,128)(2,1)} %pack.1), calls=%async_computation | async-start | bytes 4194304 | tf_op jit(solution)/shard_map/all_to_all | solution.py:421
  13.8 0.0 copy-done
  13.8 0.1 copy.20
  14.6 0.1 pad.1.clone
  14.6 0.1 reshape_squeeze.4
  14.7 0.1 broadcast_add_fusion
  14.8 0.1 broadcast_clamp_fusion
  14.9 0.1 copy.22
  15.0 0.4 and_reduce_fusion
  15.4 0.1 copy.23
  15.5 0.1 eq.53
  15.6 0.1 copy.21
  15.7 0.1 compare_reduce_fusion.1
  15.7 0.1 compare_reduce_fusion
  15.9 0.1 fusion.3
  15.9 0.1 broadcast_in_dim.18
  16.1 0.1 reshape.135
  16.2 0.1 copy.24.bias_ref
  16.3 18.1 %all-gather.1 = f32[16,1,128]{2,1,0:T(1,128)S(1)} all-gather(f32[1,1,128]{2,1,0:T(1,128)S(1)} %bitcast.12), channel_id=2, replica_groups=mesh['seq'=16,'own'=16] {'own'}, dimensions={0}, use_global_device_ids=true | all-gather | bytes 8704 | tf_op jit(solution)/shard_map/all_gather | solution.py:422
  34.4 28.4 %all-to-all-done.in_ref = bf16[16,512,128]{2,1,0:T(8,128)(2,1)S(1)} async-done(((bf16[16,512,128]{2,1,0:T(8,128)(2,1)}), bf16[16,512,128]{2,1,0:T(8,128)(2,1)S(1)}, u32[]{:S(2)}, u32[]{:S(2)}) %all-to-all-start) | async-done | bytes 2097184 | tf_op jit(solution)/shard_map/all_to_all | solution.py:421
  62.7 15.6 %forward.1 = (bf16[16,128,896]{2,1,0:T(8,128)(2,1)S(1)}, bf16[128,2048]{1,0:T(8,128)(2,1)S(1)}, bf16[16,128,128]{2,1,0:T(8,128)(2,1)S(1)}, f32[16,128,128]{2,1,0...) custom-call(s32[16,14]{1,0:T(8,128)S(1)} %get-tuple-element.26.slots_ref, ...), custom_call_target="tpu_custom_call" | custom-call | tf_op jit(solution)/shard_map/forward/pallas_call | solution.py:246
  78.3 16.5 %all_to_all.15.stat_ref = f32[16,2,2048]{2,1,0:T(2,128)S(1)} all-to-all(f32[16,2,2048]{2,1,0:T(2,128)S(1)} %get-tuple-element.20), channel_id=1, replica_groups=mesh['seq'=16,'own'=16] {'seq'}, dimensions={0} | all-to-all | bytes 524288 | tf_op jit(solution)/shard_map/all_to_all | solution.py:426
  94.8 8.0 %backward.1 = (bf16[16,384,128]{2,1,0:T(8,128)(2,1)}, f32[1,128]{1,0:T(1,128)S(1)}) custom-call(s32[16,14]{1,0:T(8,128)S(1)} %get-tuple-element.26.slots_ref, bf16[16,512,128]{2,1,0:T(8,128)(2,1)S(1)} %all-to-all-done.in_ref, bf16[16,128,896]{2,1,0:T(8,128)(2,1)S(1)} %get-tuple-element.15.probs_ref, bf16[128,2048]{1,0:T(8,128)(2,1)S(1)} %get-tuple-element.16.dense_ref, ...), custom_call_target="tpu_custom_call" | custom-call | tf_op jit(solution)/shard_map/backward/pallas_call | solution.py:366
  102.9 3.6 %all-to-all-start.2 = ((bf16[16,384,128]{2,1,0:T(8,128)(2,1)}), bf16[16,384,128]{2,1,0:T(8,128)(2,1)S(1)}, u32[]{:S(2)}, u32[]{:S(2)}) async-start(bf16[16,384,128]{2,1,0:T(8,128)(2,1)} %get-tuple-element.21), calls=%async_computation.2 | async-start | bytes 3145728 | tf_op jit(solution)/shard_map/all_to_all | solution.py:430
  106.5 18.1 %all-gather.2 = f32[16,1,128]{2,1,0:T(1,128)S(1)} all-gather(f32[1,1,128]{2,1,0:T(1,128)S(1)} %bitcast.11), channel_id=1, replica_groups=mesh['seq'=16,'own'=16] {'own'}, dimensions={0}, use_global_device_ids=true | all-gather | bytes 8704 | tf_op jit(solution)/shard_map/all_gather | solution.py:428
  124.6 0.5 broadcast_multiply_fusion
  125.1 19.2 %all-to-all-done.2.in_ref = bf16[16,384,128]{2,1,0:T(8,128)(2,1)S(1)} async-done(((bf16[16,384,128]{2,1,0:T(8,128)(2,1)}), bf16[16,384,128]{2,1,0:T(8,128)(2,1)S(1)}, u32[]{:S(2)}, u32[]{:S(2)}) %all-to-all-start.2) | async-done | bytes 1572896 | tf_op jit(solution)/shard_map/all_to_all | solution.py:430
  144.4 1.5 %unpack.1 = (bf16[1,128,2048]{2,1,0:T(8,128)(2,1)}, bf16[1,128,2048]{2,1,0:T(8,128)(2,1)}, bf16[1,128,2048]{2,1,0:T(8,128)(2,1)}) custom-call(bf16[16,384,128]{2,1,0:T(8,128)(2,1)S(1)} %all-to-all-done.2.in_ref), custom_call_target="tpu_custom_call" | custom-call | tf_op jit(solution)/shard_map/unpack/pallas_call | solution.py:104
  (10 shorter events, 0.1 us)
Async XLA Ops:
  3.6 10.2 %copy-start = (s32[1,32,3]{1,0,2:T(1,128)S(1)}, s32[1,32,3]{1,0,2:T(1,128)}, u32[]{:S(2)}) copy-start(s32[1,32,3]{1,0,2:T(1,128)} %param.15) | copy-start | bytes 1156
  3.6 10.9 %copy-start.2 = (s32[1,2]{1,0:T(1,128)S(1)}, s32[1,2]{1,0:T(1,128)}, u32[]{:S(2)}) copy-start(s32[1,2]{1,0:T(1,128)} %param.14) | copy-start | bytes 28
  3.6 12.6 %copy-start.1 = (f32[128]{0:T(128)S(1)}, f32[128]{0:T(128)}, u32[]{:S(2)}) copy-start(f32[128]{0:T(128)} %param.12) | copy-start | bytes 1540
  3.7 59.1 %all-to-all-start = ((bf16[16,512,128]{2,1,0:T(8,128)(2,1)}), bf16[16,512,128]{2,1,0:T(8,128)(2,1)S(1)}, u32[]{:S(2)}, u32[]{:S(2)}) async-start(bf16[16,512,128]{2,1,0:T(8,128)(2,1)} %pack.1), calls=%async_computation | async-start | bytes 4194304 | tf_op jit(solution)/shard_map/all_to_all | solution.py:421
  102.9 41.5 %all-to-all-start.2 = ((bf16[16,384,128]{2,1,0:T(8,128)(2,1)}), bf16[16,384,128]{2,1,0:T(8,128)(2,1)S(1)}, u32[]{:S(2)}, u32[]{:S(2)}) async-start(bf16[16,384,128]{2,1,0:T(8,128)(2,1)} %get-tuple-element.21), calls=%async_computation.2 | async-start | bytes 3145728 | tf_op jit(solution)/shard_map/all_to_all | solution.py:430

commit v4 on v3

--- a/solution.py
+++ b/solution.py
@@ -14,7 +14,8 @@
 PAIR = 2
 GLOB = 2
 GLOB_AT = PAIR + 2 * WMAX
-GROUP = 16
+PARTS = 2
+PIECES = 4
 NEG_FILL = -1e30
 EPSILON = 1e-05
 SCALE = 1.0 / math.sqrt(HDIM)
@@ -22,7 +23,7 @@
 VMEM_LIMIT = 40 * 1024 * 1024
 SUM_LOW = 2.0 ** -80
 SUM_HIGH = 2.0 ** 80
-UNPACK_VMEM_LIMIT = 16 * 1024 * 1024
+COPY_VMEM_LIMIT = 16 * 1024 * 1024
 
 NT = (((1,), (1,)), ((), ()))
 TN = (((0,), (0,)), ((), ()))
@@ -34,65 +35,77 @@
     return lax.dot_general(a, b, dims, preferred_element_type=jnp.float32)
 
 
-def pack_kernel(q_ref, k_ref, v_ref, g_ref, out_ref, stage_ref, in_sems, out_sems):
+def pack_kernel(q_ref, k_ref, v_ref, g_ref, out_ref, raw_ref, stage_ref, in_sems, out_sems):
     heads = out_ref.shape[0]
     rows = q_ref.shape[1]
+    part = rows // PARTS
+    pieces = [(slot, c) for slot in range(4) for c in range(PARTS)]
+    refs = (q_ref, k_ref, v_ref, g_ref)
     loads = [
-        [
+        pltpu.make_async_copy(
+            refs[slot].at[0, c * part:(c + 1) * part, :],
+            raw_ref.at[slot, c * part:(c + 1) * part, :],
+            in_sems.at[slot, c],
+        )
+        for slot, c in pieces
+    ]
+    for copy in loads:
+        copy.start()
+    stores = []
+    for (slot, c), copy in zip(pieces, loads):
+        copy.wait()
+        span = slice(slot * rows + c * part, slot * rows + (c + 1) * part)
+        for h in range(heads):
+            stage_ref[h, span, :] = (
+                raw_ref[slot, c * part:(c + 1) * part, h * HDIM:(h + 1) * HDIM]
+            )
+        stores.append(
             pltpu.make_async_copy(
-                ref.at[0, :, h * HDIM:(h + 1) * HDIM],
-                stage_ref.at[h, slot * rows:(slot + 1) * rows, :],
-                in_sems.at[h, slot],
-            )
-            for slot, ref in enumerate((q_ref, k_ref, v_ref, g_ref))
-        ]
-        for h in range(heads)
-    ]
-    stores = [
-        pltpu.make_async_copy(stage_ref.at[h], out_ref.at[h], out_sems.at[h]) for h in range(heads)
-    ]
-    for head_loads in loads:
-        for copy in head_loads:
-            copy.start()
-    for head_loads, store in zip(loads, stores):
-        for copy in head_loads:
-            copy.wait()
-        store.start()
-    for store in stores:
-        store.wait()
+                stage_ref.at[:, span, :], out_ref.at[:, span, :], out_sems.at[slot, c]
+            )
+        )
+        stores[-1].start()
+    for copy in stores:
+        copy.wait()
 
 
 def pack(query_rows, key_rows, value_rows, out_grad):
     _, rows, cols = query_rows.shape
     heads = cols // HDIM
+    dtype = query_rows.dtype
     return pl.pallas_call(
         pack_kernel,
-        out_shape=jax.ShapeDtypeStruct((heads, 4 * rows, HDIM), query_rows.dtype),
+        out_shape=pltpu.HBM((heads, 4 * rows, HDIM), dtype),
         in_specs=[pl.BlockSpec(memory_space=pltpu.HBM)] * 4,
         out_specs=pl.BlockSpec(memory_space=pltpu.HBM),
         scratch_shapes=[
-            pltpu.VMEM((heads, 4 * rows, HDIM), query_rows.dtype),
-            pltpu.SemaphoreType.DMA((heads, 4)),
-            pltpu.SemaphoreType.DMA((heads,)),
+            pltpu.VMEM((4, rows, cols), dtype),
+            pltpu.VMEM((heads, 4 * rows, HDIM), dtype),
+            pltpu.SemaphoreType.DMA((4, PARTS)),
+            pltpu.SemaphoreType.DMA((4, PARTS)),
         ],
         name="pack",
     )(query_rows, key_rows, value_rows, out_grad)
 
 
-def unpack_kernel(in_ref, q_ref, k_ref, v_ref, sems):
+def unpack_kernel(in_ref, q_ref, k_ref, v_ref, stage_ref, sems):
     heads = in_ref.shape[0]
     rows = q_ref.shape[1]
-    copies = [
-        pltpu.make_async_copy(
-            in_ref.at[h, slot * rows:(slot + 1) * rows, :],
-            ref.at[0, :, h * HDIM:(h + 1) * HDIM],
-            sems.at[slot, h],
-        )
-        for slot, ref in enumerate((q_ref, k_ref, v_ref))
-        for h in range(heads)
-    ]
-    for copy in copies:
-        copy.start()
+    part = rows // PARTS
+    copies = []
+    for slot, ref in enumerate((q_ref, k_ref, v_ref)):
+        for c in range(PARTS):
+            span = slice(c * part, (c + 1) * part)
+            for h in range(heads):
+                stage_ref[slot, span, h * HDIM:(h + 1) * HDIM] = (
+                    in_ref[h, slot * rows + c * part:slot * rows + (c + 1) * part, :]
+                )
+            copies.append(
+                pltpu.make_async_copy(
+                    stage_ref.at[slot, span, :], ref.at[0, span, :], sems.at[slot, c]
+                )
+            )
+            copies[-1].start()
     for copy in copies:
         copy.wait()
 
@@ -106,8 +119,11 @@
         out_shape=[shape] * 3,
         in_specs=[pl.BlockSpec(memory_space=pltpu.VMEM)],
         out_specs=[pl.BlockSpec(memory_space=pltpu.HBM)] * 3,
-        scratch_shapes=[pltpu.SemaphoreType.DMA((3, heads))],
-        compiler_params=pltpu.CompilerParams(vmem_limit_bytes=UNPACK_VMEM_LIMIT),
+        scratch_shapes=[
+            pltpu.VMEM((3, rows, heads * HDIM), exchanged.dtype),
+            pltpu.SemaphoreType.DMA((3, PARTS)),
+        ],
+        compiler_params=pltpu.CompilerParams(vmem_limit_bytes=COPY_VMEM_LIMIT),
         name="unpack",
     )(exchanged)
 
@@ -125,7 +141,7 @@
 def forward_kernel(
     slots_ref, in_ref, bias_ref, gain_ref,
     probs_ref, dense_ref, attn_ref, inv_ref, inv_dense_ref, stat_ref,
-    low_ref, high_ref,
+    part_ref,
 ):
     devs, rows4, _ = in_ref.shape
     rows = rows4 // 4
@@ -203,22 +219,13 @@
             )
         return total
 
-    def group(step, carry):
-        totals = [pair_pass(step * GROUP + u, False) for u in range(GROUP)]
-        low_ref[...] = functools.reduce(jnp.minimum, totals, low_ref[...])
-        high_ref[...] = functools.reduce(jnp.maximum, totals, high_ref[...])
-        return carry
-
     def single(pair, carry):
         pair_pass(pair, True)
         return carry
 
-    low_ref[...] = jnp.full_like(low_ref, 1.0)
-    high_ref[...] = jnp.full_like(high_ref, 1.0)
-    lax.fori_loop(0, devs // GROUP, group, 0)
-    total = dense_pass(False)
-    low = jnp.min(jnp.minimum(low_ref[...], total))
-    high = jnp.max(jnp.maximum(high_ref[...], total))
+    totals = [pair_pass(pair, False) for pair in range(devs)] + [dense_pass(False)]
+    low = jnp.min(functools.reduce(jnp.minimum, totals))
+    high = jnp.max(functools.reduce(jnp.maximum, totals))
     in_range = (low > SUM_LOW) & (high < SUM_HIGH)
 
     @pl.when(jnp.logical_not(in_range))
@@ -231,9 +238,10 @@
         grad = in_ref[i, 3 * rows:4 * rows, :].astype(jnp.float32) * gain_ref[...]
         square = jnp.sum((attn * attn).T, axis=0, keepdims=True)
         inner = jnp.sum((grad * attn).T, axis=0, keepdims=True)
-        stats = jnp.concatenate([square, inner], axis=0)
-        for d in range(devs):
-            stat_ref[d, :, i * rows:(i + 1) * rows] = stats
+        part_ref[i:i + 1, :] = jnp.concatenate([square, inner], axis=1)
+    stats = part_ref[...].astype(stat_ref.dtype)
+    for d in range(devs):
+        stat_ref[d] = stats
 
 
 def forward(slots, exchanged, bias, gain_row):
@@ -251,11 +259,11 @@
             jax.ShapeDtypeStruct((devs, rows, HDIM), jnp.bfloat16),
             jax.ShapeDtypeStruct((devs, rows, HDIM), jnp.float32),
             jax.ShapeDtypeStruct((GLOB * BLK, HDIM), jnp.float32),
-            jax.ShapeDtypeStruct((devs, 2, seq), jnp.float32),
+            jax.ShapeDtypeStruct((devs, devs, 2 * rows), jnp.bfloat16),
         ],
         in_specs=[smem, vmem, vmem, vmem],
         out_specs=[vmem] * 6,
-        scratch_shapes=[pltpu.VMEM((rows, HDIM), jnp.float32)] * 2,
+        scratch_shapes=[pltpu.VMEM((devs, 2 * rows), jnp.float32)],
         compiler_params=pltpu.CompilerParams(vmem_limit_bytes=VMEM_LIMIT),
         name="forward",
     )(slots, exchanged, bias, gain_row)
@@ -273,17 +281,16 @@
     count = slots_ref.shape[1]
     globs = GLOB
 
-    stats = stat_ref[0]
+    stats = stat_ref[0].astype(jnp.float32)
     for d in range(1, devs):
-        stats = stats + stat_ref[d]
+        stats = stats + stat_ref[d].astype(jnp.float32)
     stats = stats * (1.0 / (devs * HDIM))
-    inv_rms = lax.rsqrt(stats[0:1] + EPSILON)
-    shrink = inv_rms * inv_rms * stats[1:2]
+    inv_rms = lax.rsqrt(stats[:, :rows] + EPSILON)
+    shrink = inv_rms * inv_rms * stats[:, rows:]
     gain = jnp.zeros((8, HDIM), jnp.float32)
     for i in range(devs):
-        span = slice(i * rows, (i + 1) * rows)
-        factor = jnp.broadcast_to(inv_rms[:, span], (HDIM, rows)).T
-        minus = jnp.broadcast_to(shrink[:, span], (HDIM, rows)).T
+        factor = jnp.broadcast_to(inv_rms[i:i + 1], (HDIM, rows)).T
+        minus = jnp.broadcast_to(shrink[i:i + 1], (HDIM, rows)).T
         attn = attn_ref[i].astype(jnp.float32)
         grad = in_ref[i, 3 * rows:4 * rows, :].astype(jnp.float32)
         grad_ref[i] = factor * (gain_ref[...] * grad - attn * minus)
@@ -319,26 +326,21 @@
         dq_dense = dq_dense + dot(ds, keys)
         acc_ref[c * step:(c + 1) * step, :] = dot(jnp.concatenate([probs, ds], axis=0), both, TN)
 
-    def group(step, carry):
-        for u in range(GROUP):
-            pair = step * GROUP + u
-            ids = [slots_ref[pair, t] for t in range(count)]
-            values = jnp.concatenate([block_of(in_ref, b, 2) for b in ids], axis=0)
-            keys = jnp.concatenate([block_of(in_ref, b, 1) for b in ids], axis=0)
-            q = in_ref[pair, 0:rows, :]
-            low = (grad_ref[pair] * inv_ref[pair]).astype(jnp.bfloat16)
-            probs = probs_ref[pair]
-            dots = row_dot(low, attn_ref[pair])
-            ds = (probs.astype(jnp.float32) * (dot(low, values, NT) - dots)).astype(jnp.bfloat16)
-            stage_ref[pair, 0:rows, :] = (dot(ds, keys) * SCALE).astype(jnp.bfloat16)
-            both = dot(jnp.concatenate([probs, ds], axis=0), side(low, q), TN)
-            for t, block in enumerate(ids):
-                acc_ref[pl.ds(pl.multiple_of(block * BLK, BLK), BLK), :] += (
-                    both[t * BLK:(t + 1) * BLK]
-                )
-        return carry
-
-    lax.fori_loop(0, devs // GROUP, group, 0)
+    for pair in range(devs):
+        ids = [slots_ref[pair, t] for t in range(count)]
+        values = jnp.concatenate([block_of(in_ref, b, 2) for b in ids], axis=0)
+        keys = jnp.concatenate([block_of(in_ref, b, 1) for b in ids], axis=0)
+        q = in_ref[pair, 0:rows, :]
+        low = (grad_ref[pair] * inv_ref[pair]).astype(jnp.bfloat16)
+        probs = probs_ref[pair]
+        dots = row_dot(low, attn_ref[pair])
+        ds = (probs.astype(jnp.float32) * (dot(low, values, NT) - dots)).astype(jnp.bfloat16)
+        stage_ref[pair, 0:rows, :] = (dot(ds, keys) * SCALE).astype(jnp.bfloat16)
+        both = dot(jnp.concatenate([probs, ds], axis=0), side(low, q), TN)
+        for t, block in enumerate(ids):
+            acc_ref[pl.ds(pl.multiple_of(block * BLK, BLK), BLK), :] += (
+                both[t * BLK:(t + 1) * BLK]
+            )
 
     per = rows // BLK
     dq_dense = (dq_dense * SCALE).astype(jnp.bfloat16)
@@ -346,12 +348,20 @@
         stage_ref[block // per, pl.ds(pl.multiple_of((block % per) * BLK, BLK), BLK), :] = (
             dq_dense[t * BLK:(t + 1) * BLK]
         )
-    copies = []
-    for i in range(devs):
-        span = slice(i * rows, (i + 1) * rows)
-        stage_ref[i, rows:2 * rows, :] = (acc_ref[span, HDIM:] * SCALE).astype(jnp.bfloat16)
-        stage_ref[i, 2 * rows:3 * rows, :] = acc_ref[span, :HDIM].astype(jnp.bfloat16)
-        copies.append(pltpu.make_async_copy(stage_ref.at[i], out_ref.at[i], sems.at[i]))
+    copies = [
+        pltpu.make_async_copy(stage_ref.at[:, 0:rows, :], out_ref.at[:, 0:rows, :], sems.at[0])
+    ]
+    copies[0].start()
+    group = devs // PIECES
+    for n in range(PIECES):
+        for i in range(n * group, (n + 1) * group):
+            span = slice(i * rows, (i + 1) * rows)
+            stage_ref[i, rows:2 * rows, :] = (acc_ref[span, HDIM:] * SCALE).astype(jnp.bfloat16)
+            stage_ref[i, 2 * rows:3 * rows, :] = acc_ref[span, :HDIM].astype(jnp.bfloat16)
+        part = (slice(n * group, (n + 1) * group), slice(rows, 3 * rows))
+        copies.append(
+            pltpu.make_async_copy(stage_ref.at[*part], out_ref.at[*part], sems.at[n + 1])
+        )
         copies[-1].start()
     for copy in copies:
         copy.wait()
@@ -375,7 +385,7 @@
             pltpu.VMEM((devs, rows, HDIM), jnp.float32),
             pltpu.VMEM((seq, 2 * HDIM), jnp.float32),
             pltpu.VMEM((devs, 3 * rows, HDIM), jnp.bfloat16),
-            pltpu.SemaphoreType.DMA((devs,)),
+            pltpu.SemaphoreType.DMA((PIECES + 1,)),
         ],
         compiler_params=pltpu.CompilerParams(vmem_limit_bytes=VMEM_LIMIT),
         name="backward",

time: 146 us -> 143 us (0.979)
  blocking collectives: 52.6 us -> 50.1 us
    all_to_all x1, blocking collectives: 16.5 us -> 13.9 us  [body(): stats = exchange(stats)]
where the time goes in v4:
time: 143 us
  blocking collectives  50.1 us (35%)
  waiting for transfers between devices  47.7 us (33%)
  Pallas kernels  27.2 us (19%)
  starting transfers between devices  13.7 us (10%)
  between operations  1.58 us (1%)
    all_to_all x1, waiting for transfers between devices, body(): exchanged = exchange(pack(query_rows, key_rows, value_rows, out_grad))  28.4 us
    all_to_all x1, waiting for transfers between devices, body(): out_query, out_key, out_value = unpack(exchange(grads))  19.3 us
    all_gather x1, blocking collectives, body(): gains = lax.all_gather(norm_gains, 'own')  18.1 us
    all_gather x1, blocking collectives, body(): gain_terms = lax.all_gather(gain_part.reshape(-1), 'own')  18.1 us
    pallas_call x1, Pallas kernels, forward(): pl.pallas_call(forward_kernel, out_shape=[jax.ShapeDtypeStruct((devs, row...  15.6 us
    all_to_all x1, blocking collectives, body(): stats = exchange(stats)  13.9 us
    all_to_all x1, starting transfers between devices, body(): exchanged = exchange(pack(query_rows, key_rows, value_rows, out_grad))  10.1 us
    pallas_call x1, Pallas kernels, backward(): pl.pallas_call(backward_kernel, out_shape=[pltpu.HBM((devs, 3 * rows, HDI...  7.85 us
  transfers between devices with their start and end apart: 2, of which 2 were waited for; matrix products, arithmetic and copies ran while one was open for 2% of the time, Pallas kernels for 0%

profile of v4, /device:TPU:1, one launch (start us, length us, event | category | flops | bytes accessed | tf_op | source)
XLA Modules:
  0.0 142.6 jit_solution(14432243342364648544)
XLA Ops:
  0.6 2.5 %pack.1 = bf16[16,512,128]{2,1,0:T(8,128)(2,1)} custom-call(bf16[1,128,2048]{2,1,0:T(8,128)(2,1)} %q_ref.1, bf16[1,128,2048]{2,1,0:T(8,128)(2,1)} %k_ref.1, bf16[1,128,2048]{2,1,0:T(8,128)(2,1)} %v_ref.1, bf16[1,128,2048]{2,1,0:T(8,128)(2,1)} %g_ref.1), custom_call_target="tpu_custom_call" | custom-call | tf_op jit(solution)/shard_map/pack/pallas_call | solution.py:76
  3.2 0.0 copy-start
  3.2 0.0 copy-start.2
  3.2 0.0 copy-start.1
  3.2 10.1 %all-to-all-start = ((bf16[16,512,128]{2,1,0:T(8,128)(2,1)}), bf16[16,512,128]{2,1,0:T(8,128)(2,1)S(1)}, u32[]{:S(2)}, u32[]{:S(2)}) async-start(bf16[16,512,128]{2,1,0:T(8,128)(2,1)} %pack.1), calls=%async_computation | async-start | bytes 4194304 | tf_op jit(solution)/shard_map/all_to_all | solution.py:431
  13.3 0.0 copy-done
  13.3 0.1 copy.20
  14.1 0.1 pad.1.clone
  14.2 0.1 reshape_squeeze.4
  14.2 0.1 broadcast_add_fusion
  14.3 0.1 broadcast_clamp_fusion
  14.4 0.1 copy.22
  14.5 0.4 and_reduce_fusion
  14.9 0.1 copy.23
  15.0 0.1 eq.53
  15.1 0.1 copy.21
  15.2 0.1 compare_reduce_fusion.1
  15.3 0.1 compare_reduce_fusion
  15.4 0.1 fusion.3
  15.5 0.1 broadcast_in_dim.18
  15.6 0.1 reshape.135
  15.7 0.1 copy.24.bias_ref
  15.8 18.1 %all-gather.1 = f32[16,1,128]{2,1,0:T(1,128)S(1)} all-gather(f32[1,1,128]{2,1,0:T(1,128)S(1)} %bitcast.12), channel_id=2, replica_groups=mesh['seq'=16,'own'=16] {'own'}, dimensions={0}, use_global_device_ids=true | all-gather | bytes 8704 | tf_op jit(solution)/shard_map/all_gather | solution.py:432
  33.9 28.4 %all-to-all-done.in_ref = bf16[16,512,128]{2,1,0:T(8,128)(2,1)S(1)} async-done(((bf16[16,512,128]{2,1,0:T(8,128)(2,1)}), bf16[16,512,128]{2,1,0:T(8,128)(2,1)S(1)}, u32[]{:S(2)}, u32[]{:S(2)}) %all-to-all-start) | async-done | bytes 2097184 | tf_op jit(solution)/shard_map/all_to_all | solution.py:431
  62.3 15.6 %forward.1 = (bf16[16,128,896]{2,1,0:T(8,128)(2,1)S(1)}, bf16[128,2048]{1,0:T(8,128)(2,1)S(1)}, bf16[16,128,128]{2,1,0:T(8,128)(2,1)S(1)}, f32[16,128,128]{2,1,0...) custom-call(s32[16,14]{1,0:T(8,128)S(1)} %get-tuple-element.26.slots_ref, ...), custom_call_target="tpu_custom_call" | custom-call | tf_op jit(solution)/shard_map/forward/pallas_call | solution.py:254
  77.9 13.9 %all_to_all.15.stat_ref = bf16[16,16,256]{2,1,0:T(8,128)(2,1)S(1)} all-to-all(bf16[16,16,256]{2,1,0:T(8,128)(2,1)S(1)} %get-tuple-element.20), channel_id=1, replica_groups=mesh['seq'=16,'own'=16] {'seq'}, dimensions={0} | all-to-all | bytes 262144 | tf_op jit(solution)/shard_map/all_to_all | solution.py:436
  91.8 7.8 %backward.1 = (bf16[16,384,128]{2,1,0:T(8,128)(2,1)}, f32[1,128]{1,0:T(1,128)S(1)}) custom-call(s32[16,14]{1,0:T(8,128)S(1)} %get-tuple-element.26.slots_ref, bf16[16,512,128]{2,1,0:T(8,128)(2,1)S(1)} %all-to-all-done.in_ref, bf16[16,128,896]{2,1,0:T(8,128)(2,1)S(1)} %get-tuple-element.15.probs_ref, bf16[128,2048]{1,0:T(8,128)(2,1)S(1)} %get-tuple-element.16.dense_ref, ...), custom_call_target="tpu_custom_call" | custom-call | tf_op jit(solution)/shard_map/backward/pallas_call | solution.py:376
  99.7 3.6 %all-to-all-start.2 = ((bf16[16,384,128]{2,1,0:T(8,128)(2,1)}), bf16[16,384,128]{2,1,0:T(8,128)(2,1)S(1)}, u32[]{:S(2)}, u32[]{:S(2)}) async-start(bf16[16,384,128]{2,1,0:T(8,128)(2,1)} %get-tuple-element.21), calls=%async_computation.2 | async-start | bytes 3145728 | tf_op jit(solution)/shard_map/all_to_all | solution.py:440
  103.3 18.1 %all-gather.2 = f32[16,1,128]{2,1,0:T(1,128)S(1)} all-gather(f32[1,1,128]{2,1,0:T(1,128)S(1)} %bitcast.11), channel_id=1, replica_groups=mesh['seq'=16,'own'=16] {'own'}, dimensions={0}, use_global_device_ids=true | all-gather | bytes 8704 | tf_op jit(solution)/shard_map/all_gather | solution.py:438
  121.4 0.5 broadcast_multiply_fusion
  121.9 19.3 %all-to-all-done.2.in_ref = bf16[16,384,128]{2,1,0:T(8,128)(2,1)S(1)} async-done(((bf16[16,384,128]{2,1,0:T(8,128)(2,1)}), bf16[16,384,128]{2,1,0:T(8,128)(2,1)S(1)}, u32[]{:S(2)}, u32[]{:S(2)}) %all-to-all-start.2) | async-done | bytes 1572896 | tf_op jit(solution)/shard_map/all_to_all | solution.py:440
  141.2 1.2 unpack.1
  (10 shorter events, 0.1 us)
Async XLA Ops:
  3.2 10.2 %copy-start = (s32[1,32,3]{1,0,2:T(1,128)S(1)}, s32[1,32,3]{1,0,2:T(1,128)}, u32[]{:S(2)}) copy-start(s32[1,32,3]{1,0,2:T(1,128)} %param.15) | copy-start | bytes 1156
  3.2 10.9 %copy-start.2 = (s32[1,2]{1,0:T(1,128)S(1)}, s32[1,2]{1,0:T(1,128)}, u32[]{:S(2)}) copy-start(s32[1,2]{1,0:T(1,128)} %param.14) | copy-start | bytes 28
  3.2 12.6 %copy-start.1 = (f32[128]{0:T(128)S(1)}, f32[128]{0:T(128)}, u32[]{:S(2)}) copy-start(f32[128]{0:T(128)} %param.12) | copy-start | bytes 1540
  3.2 59.1 %all-to-all-start = ((bf16[16,512,128]{2,1,0:T(8,128)(2,1)}), bf16[16,512,128]{2,1,0:T(8,128)(2,1)S(1)}, u32[]{:S(2)}, u32[]{:S(2)}) async-start(bf16[16,512,128]{2,1,0:T(8,128)(2,1)} %pack.1), calls=%async_computation | async-start | bytes 4194304 | tf_op jit(solution)/shard_map/all_to_all | solution.py:431
  99.7 41.5 %all-to-all-start.2 = ((bf16[16,384,128]{2,1,0:T(8,128)(2,1)}), bf16[16,384,128]{2,1,0:T(8,128)(2,1)S(1)}, u32[]{:S(2)}, u32[]{:S(2)}) async-start(bf16[16,384,128]{2,1,0:T(8,128)(2,1)} %get-tuple-element.21), calls=%async_computation.2 | async-start | bytes 3145728 | tf_op jit(solution)/shard_map/all_to_all | solution.py:440

commit v5 on v4

--- a/solution.py
+++ b/solution.py
@@ -15,7 +15,7 @@
 GLOB = 2
 GLOB_AT = PAIR + 2 * WMAX
 PARTS = 2
-PIECES = 4
+PIECES = 2
 NEG_FILL = -1e30
 EPSILON = 1e-05
 SCALE = 1.0 / math.sqrt(HDIM)
@@ -316,11 +316,11 @@
     attn = jnp.concatenate([block_of(attn_ref, b, 0) for b in blocks], axis=0)
     both = side(low, q)
     dots = row_dot(low, attn)
-    step = 512
+    step = 1024
     dq_dense = jnp.zeros((globs * BLK, HDIM), jnp.float32)
     for c in range(seq // step):
-        values = in_ref[c * 4:(c + 1) * 4, 2 * rows:3 * rows, :].reshape(step, HDIM)
-        keys = in_ref[c * 4:(c + 1) * 4, rows:2 * rows, :].reshape(step, HDIM)
+        values = in_ref[c * 8:(c + 1) * 8, 2 * rows:3 * rows, :].reshape(step, HDIM)
+        keys = in_ref[c * 8:(c + 1) * 8, rows:2 * rows, :].reshape(step, HDIM)
         probs = dense_ref[:, c * step:(c + 1) * step]
         ds = (probs.astype(jnp.float32) * (dot(low, values, NT) - dots)).astype(jnp.bfloat16)
         dq_dense = dq_dense + dot(ds, keys)

time: 143 us -> 143 us (level)
  no operation moved by 1% of the time
where the time goes in v5:
time: 143 us; the launch traced here: 142 us
  blocking collectives  50.1 us (35%)
  waiting for transfers between devices  47.7 us (33%)
  Pallas kernels  27.1 us (19%)
  starting transfers between devices  13.7 us (10%)
  between operations  1.58 us (1%)
    all_to_all x1, waiting for transfers between devices, body(): exchanged = exchange(pack(query_rows, key_rows, value_rows, out_grad))  28.4 us
    all_to_all x1, waiting for transfers between devices, body(): out_query, out_key, out_value = unpack(exchange(grads))  19.3 us
    all_gather x1, blocking collectives, body(): gains = lax.all_gather(norm_gains, 'own')  18.1 us
    all_gather x1, blocking collectives, body(): gain_terms = lax.all_gather(gain_part.reshape(-1), 'own')  18.1 us
    pallas_call x1, Pallas kernels, forward(): pl.pallas_call(forward_kernel, out_shape=[jax.ShapeDtypeStruct((devs, row...  15.6 us
    all_to_all x1, blocking collectives, body(): stats = exchange(stats)  13.9 us
    all_to_all x1, starting transfers between devices, body(): exchanged = exchange(pack(query_rows, key_rows, value_rows, out_grad))  10.1 us
    pallas_call x1, Pallas kernels, backward(): pl.pallas_call(backward_kernel, out_shape=[pltpu.HBM((devs, 3 * rows, HDI...  7.74 us
  transfers between devices with their start and end apart: 2, of which 2 were waited for; matrix products, arithmetic and copies ran while one was open for 2% of the time, Pallas kernels for 0%

profile of v5, /device:TPU:1, one launch (start us, length us, event | category | flops | bytes accessed | tf_op | source)
XLA Modules:
  0.0 142.5 jit_solution(15541689111526077345)
XLA Ops:
  0.6 2.5 %pack.1 = bf16[16,512,128]{2,1,0:T(8,128)(2,1)} custom-call(bf16[1,128,2048]{2,1,0:T(8,128)(2,1)} %q_ref.1, bf16[1,128,2048]{2,1,0:T(8,128)(2,1)} %k_ref.1, bf16[1,128,2048]{2,1,0:T(8,128)(2,1)} %v_ref.1, bf16[1,128,2048]{2,1,0:T(8,128)(2,1)} %g_ref.1), custom_call_target="tpu_custom_call" | custom-call | tf_op jit(solution)/shard_map/pack/pallas_call | solution.py:76
  3.2 0.0 copy-start
  3.2 0.0 copy-start.2
  3.2 0.0 copy-start.1
  3.2 10.1 %all-to-all-start = ((bf16[16,512,128]{2,1,0:T(8,128)(2,1)}), bf16[16,512,128]{2,1,0:T(8,128)(2,1)S(1)}, u32[]{:S(2)}, u32[]{:S(2)}) async-start(bf16[16,512,128]{2,1,0:T(8,128)(2,1)} %pack.1), calls=%async_computation | async-start | bytes 4194304 | tf_op jit(solution)/shard_map/all_to_all | solution.py:431
  13.3 0.0 copy-done
  13.3 0.1 copy.20
  14.1 0.1 pad.1.clone
  14.2 0.1 reshape_squeeze.4
  14.2 0.1 broadcast_add_fusion
  14.3 0.1 broadcast_clamp_fusion
  14.4 0.1 copy.22
  14.5 0.4 and_reduce_fusion
  14.9 0.1 copy.23
  15.0 0.1 eq.53
  15.1 0.1 copy.21
  15.2 0.1 compare_reduce_fusion.1
  15.3 0.1 compare_reduce_fusion
  15.4 0.1 fusion.3
  15.5 0.1 broadcast_in_dim.18
  15.6 0.1 reshape.135
  15.7 0.1 copy.24.bias_ref
  15.8 18.1 %all-gather.1 = f32[16,1,128]{2,1,0:T(1,128)S(1)} all-gather(f32[1,1,128]{2,1,0:T(1,128)S(1)} %bitcast.12), channel_id=2, replica_groups=mesh['seq'=16,'own'=16] {'own'}, dimensions={0}, use_global_device_ids=true | all-gather | bytes 8704 | tf_op jit(solution)/shard_map/all_gather | solution.py:432
  33.9 28.4 %all-to-all-done.in_ref = bf16[16,512,128]{2,1,0:T(8,128)(2,1)S(1)} async-done(((bf16[16,512,128]{2,1,0:T(8,128)(2,1)}), bf16[16,512,128]{2,1,0:T(8,128)(2,1)S(1)}, u32[]{:S(2)}, u32[]{:S(2)}) %all-to-all-start) | async-done | bytes 2097184 | tf_op jit(solution)/shard_map/all_to_all | solution.py:431
  62.3 15.6 %forward.1 = (bf16[16,128,896]{2,1,0:T(8,128)(2,1)S(1)}, bf16[128,2048]{1,0:T(8,128)(2,1)S(1)}, bf16[16,128,128]{2,1,0:T(8,128)(2,1)S(1)}, f32[16,128,128]{2,1,0...) custom-call(s32[16,14]{1,0:T(8,128)S(1)} %get-tuple-element.26.slots_ref, ...), custom_call_target="tpu_custom_call" | custom-call | tf_op jit(solution)/shard_map/forward/pallas_call | solution.py:254
  77.9 13.9 %all_to_all.15.stat_ref = bf16[16,16,256]{2,1,0:T(8,128)(2,1)S(1)} all-to-all(bf16[16,16,256]{2,1,0:T(8,128)(2,1)S(1)} %get-tuple-element.20), channel_id=1, replica_groups=mesh['seq'=16,'own'=16] {'seq'}, dimensions={0} | all-to-all | bytes 262144 | tf_op jit(solution)/shard_map/all_to_all | solution.py:436
  91.8 7.7 %backward.1 = (bf16[16,384,128]{2,1,0:T(8,128)(2,1)}, f32[1,128]{1,0:T(1,128)S(1)}) custom-call(s32[16,14]{1,0:T(8,128)S(1)} %get-tuple-element.26.slots_ref, bf16[16,512,128]{2,1,0:T(8,128)(2,1)S(1)} %all-to-all-done.in_ref, bf16[16,128,896]{2,1,0:T(8,128)(2,1)S(1)} %get-tuple-element.15.probs_ref, bf16[128,2048]{1,0:T(8,128)(2,1)S(1)} %get-tuple-element.16.dense_ref, ...), custom_call_target="tpu_custom_call" | custom-call | tf_op jit(solution)/shard_map/backward/pallas_call | solution.py:376
  99.6 3.6 %all-to-all-start.2 = ((bf16[16,384,128]{2,1,0:T(8,128)(2,1)}), bf16[16,384,128]{2,1,0:T(8,128)(2,1)S(1)}, u32[]{:S(2)}, u32[]{:S(2)}) async-start(bf16[16,384,128]{2,1,0:T(8,128)(2,1)} %get-tuple-element.21), calls=%async_computation.2 | async-start | bytes 3145728 | tf_op jit(solution)/shard_map/all_to_all | solution.py:440
  103.2 18.1 %all-gather.2 = f32[16,1,128]{2,1,0:T(1,128)S(1)} all-gather(f32[1,1,128]{2,1,0:T(1,128)S(1)} %bitcast.11), channel_id=1, replica_groups=mesh['seq'=16,'own'=16] {'own'}, dimensions={0}, use_global_device_ids=true | all-gather | bytes 8704 | tf_op jit(solution)/shard_map/all_gather | solution.py:438
  121.3 0.5 broadcast_multiply_fusion
  121.8 19.3 %all-to-all-done.2.in_ref = bf16[16,384,128]{2,1,0:T(8,128)(2,1)S(1)} async-done(((bf16[16,384,128]{2,1,0:T(8,128)(2,1)}), bf16[16,384,128]{2,1,0:T(8,128)(2,1)S(1)}, u32[]{:S(2)}, u32[]{:S(2)}) %all-to-all-start.2) | async-done | bytes 1572896 | tf_op jit(solution)/shard_map/all_to_all | solution.py:440
  141.1 1.2 unpack.1
  (10 shorter events, 0.1 us)
Async XLA Ops:
  3.2 10.2 %copy-start = (s32[1,32,3]{1,0,2:T(1,128)S(1)}, s32[1,32,3]{1,0,2:T(1,128)}, u32[]{:S(2)}) copy-start(s32[1,32,3]{1,0,2:T(1,128)} %param.15) | copy-start | bytes 1156
  3.2 10.9 %copy-start.2 = (s32[1,2]{1,0:T(1,128)S(1)}, s32[1,2]{1,0:T(1,128)}, u32[]{:S(2)}) copy-start(s32[1,2]{1,0:T(1,128)} %param.14) | copy-start | bytes 28
  3.2 12.6 %copy-start.1 = (f32[128]{0:T(128)S(1)}, f32[128]{0:T(128)}, u32[]{:S(2)}) copy-start(f32[128]{0:T(128)} %param.12) | copy-start | bytes 1540
  3.2 59.1 %all-to-all-start = ((bf16[16,512,128]{2,1,0:T(8,128)(2,1)}), bf16[16,512,128]{2,1,0:T(8,128)(2,1)S(1)}, u32[]{:S(2)}, u32[]{:S(2)}) async-start(bf16[16,512,128]{2,1,0:T(8,128)(2,1)} %pack.1), calls=%async_computation | async-start | bytes 4194304 | tf_op jit(solution)/shard_map/all_to_all | solution.py:431
  99.6 41.5 %all-to-all-start.2 = ((bf16[16,384,128]{2,1,0:T(8,128)(2,1)}), bf16[16,384,128]{2,1,0:T(8,128)(2,1)S(1)}, u32[]{:S(2)}, u32[]{:S(2)}) async-start(bf16[16,384,128]{2,1,0:T(8,128)(2,1)} %get-tuple-element.21), calls=%async_computation.2 | async-start | bytes 3145728 | tf_op jit(solution)/shard_map/all_to_all | solution.py:440
